TPU v7x, 128 devices: a whole 4x4x4 slice. The times are simulated.
128 devices in a mesh: member: 16 (over y_lo, x, core), fsdp: 8 (over y_hi, z).
Axes of the slice: x: 4, y: 4 (y_hi: 2, y_lo: 2; y = y_hi * 2 + y_lo), z: 4, core: 2. Of those that a mesh axis runs over, the one named last changes fastest.
Arguments:
- tokens: bfloat16 [16, 1024, 1536], P('member', 'fsdp'), may hold values from -48 to 48
- upstream: bfloat16 [16, 1024, 1536], P('member', 'fsdp'), may hold values from -6 to 6
- gate_weight: bfloat16 [16, 1536, 6144], P('member', None, 'fsdp'), may hold values from -0.15625 to 0.15625
- up_weight: bfloat16 [16, 1536, 6144], P('member', None, 'fsdp'), may hold values from -0.15625 to 0.15625
- down_weight: bfloat16 [16, 6144, 1536], P('member', 'fsdp'), may hold values from -0.078125 to 0.078125
- norm_gain: bfloat16 [16, 1536], P('member'), may hold values from 0.099609375 to 1.8984375
- stale_gate: bfloat16 [16, 1536, 6144], P('member', None, 'fsdp'), may hold values from -0.15625 to 0.15625
- stale_up: bfloat16 [16, 1536, 6144], P('member', None, 'fsdp'), may hold values from -0.15625 to 0.15625
- stale_down: bfloat16 [16, 6144, 1536], P('member', 'fsdp'), may hold values from -0.078125 to 0.078125
- stale_gain: bfloat16 [16, 1536], P('member'), may hold values from 0.099609375 to 1.8984375
Outputs:
- grad_tokens: bfloat16 [16, 1024, 1536], P('member', 'fsdp')
- grad_gate: bfloat16 [16, 1536, 6144], P('member', None, 'fsdp')
- grad_up: bfloat16 [16, 1536, 6144], P('member', None, 'fsdp')
- grad_down: bfloat16 [16, 6144, 1536], P('member', 'fsdp')
- grad_gain: float32 [16, 1536], P('member')
All inputs are finite; a program needn't handle non-finite values.
Results may differ from a plain program's by a relative error of at most 0.02.
Values may be sent and summed in bfloat16 or wider, within the bound.
A program may use at most 128 MiB of HBM per device.

v0:
```python
import jax
import jax.numpy as jnp
from jax import lax
from jax.sharding import PartitionSpec as P

EPS = 1e-05
AGREE = 1.0


def shifted(value, axis, steps):
    count = lax.axis_size(axis)
    pairs = [(source, (source + steps) % count) for source in range(count)]
    return lax.ppermute(value, axis, pairs)


def normalize(rows_in):
    values = rows_in.astype(jnp.float32)
    inverse = lax.rsqrt(jnp.mean(values * values, axis=-1, keepdims=True) + EPS)
    return (values * inverse, inverse)


def project_up(inputs, gate_weight, up_weight):
    gate_value = jnp.dot(inputs, gate_weight, preferred_element_type=jnp.float32)
    up_value = jnp.dot(inputs, up_weight, preferred_element_type=jnp.float32)
    hidden = (jax.nn.silu(gate_value) * up_value).astype(jnp.bfloat16)
    return (gate_value, up_value, hidden)


def shards(
    tokens,
    upstream,
    gate_weight,
    up_weight,
    down_weight,
    norm_gain,
    stale_gate,
    stale_up,
    stale_down,
    stale_gain,
):
    own_rows = tokens[0]
    gathered = lax.all_gather(own_rows, "fsdp", axis=0, tiled=True)
    normed, inverse = normalize(gathered)
    gain_value = norm_gain[0].astype(jnp.float32)
    inputs = (normed * gain_value).astype(jnp.bfloat16)
    gate_value, up_value, hidden = project_up(inputs, gate_weight[0], up_weight[0])
    own_down = down_weight[0]
    peer_gate, peer_up, peer_down, peer_gain = shifted(
        (stale_gate[0], stale_up[0], stale_down[0], stale_gain[0]), "member", 1
    )
    peer_inputs = (normed * peer_gain.astype(jnp.float32)).astype(jnp.bfloat16)
    peer_hidden = project_up(peer_inputs, peer_gate, peer_up)[2]
    out_gap = lax.psum_scatter(
        (
            jnp.dot(hidden, own_down, preferred_element_type=jnp.float32)
            - jnp.dot(peer_hidden, peer_down, preferred_element_type=jnp.float32)
        ).astype(jnp.bfloat16),
        "fsdp",
        scatter_dimension=0,
        tiled=True,
    ).astype(jnp.float32)
    grad_out = (upstream[0].astype(jnp.float32) + AGREE * out_gap).astype(jnp.bfloat16)
    grad_rows = lax.all_gather(grad_out, "fsdp", axis=0, tiled=True)
    grad_hidden = jnp.einsum("rd,fd->rf", grad_rows, own_down, preferred_element_type=jnp.float32)
    sigma = jax.nn.sigmoid(gate_value)
    grad_gate_pre = (grad_hidden * up_value * sigma * (1.0 + gate_value * (1.0 - sigma))).astype(
        jnp.bfloat16
    )
    grad_up_pre = (grad_hidden * jax.nn.silu(gate_value)).astype(jnp.bfloat16)
    grad_down = jnp.einsum(
        "rf,rd->fd", hidden, grad_rows, preferred_element_type=jnp.float32
    ).astype(jnp.bfloat16)
    grad_gate = jnp.einsum(
        "rd,rf->df", inputs, grad_gate_pre, preferred_element_type=jnp.float32
    ).astype(jnp.bfloat16)
    grad_up = jnp.einsum(
        "rd,rf->df", inputs, grad_up_pre, preferred_element_type=jnp.float32
    ).astype(jnp.bfloat16)
    from_gate = jnp.einsum(
        "rf,df->rd", grad_gate_pre, gate_weight[0], preferred_element_type=jnp.float32
    )
    from_up = jnp.einsum("rf,df->rd", grad_up_pre, up_weight[0], preferred_element_type=jnp.float32)
    grad_inputs = lax.psum_scatter(
        (from_gate + from_up).astype(jnp.bfloat16), "fsdp", scatter_dimension=0, tiled=True
    ).astype(jnp.float32)
    own_normed, own_inverse = normalize(own_rows)
    grad_gain = lax.psum(jnp.sum(grad_inputs * own_normed, axis=0), "fsdp")
    grad_normed = grad_inputs * gain_value
    grad_tokens = grad_out.astype(jnp.float32) + own_inverse * (
        grad_normed - own_normed * jnp.mean(grad_normed * own_normed, axis=-1, keepdims=True)
    )
    return (
        grad_tokens.astype(jnp.bfloat16)[None],
        grad_gate[None],
        grad_up[None],
        grad_down[None],
        grad_gain[None],
    )


def solution(mesh):
    in_specs = (
        P("member", "fsdp", None),
        P("member", "fsdp", None),
        P("member", None, "fsdp"),
        P("member", None, "fsdp"),
        P("member", "fsdp", None),
        P("member", None),
        P("member", None, "fsdp"),
        P("member", None, "fsdp"),
        P("member", "fsdp", None),
        P("member", None),
    )
    out_specs = (
        P("member", "fsdp", None),
        P("member", None, "fsdp"),
        P("member", None, "fsdp"),
        P("member", "fsdp", None),
        P("member", None),
    )
    return jax.shard_map(shards, mesh=mesh, in_specs=in_specs, out_specs=out_specs, check_vma=False)
```

profile of v0, /device:TPU:0, one launch (start us, length us, event | category | flops | bytes accessed | tf_op | source)
XLA Modules:
  0.0 441.0 jit_solution(5566591274471457248)
XLA Ops:
  7.2 0.7 all-gather.6.cloned.1.call-update
  8.0 1.7 collective-permute-start.2
  9.7 0.7 reduce.1
  10.4 0.1 collective-permute-start
  10.6 1.5 collective-permute-start.1
  12.1 0.7 convert_reduce_fusion
  12.8 51.3 %collective-permute-done = bf16[1536]{0:T(1024)(128)(2,1)S(1)} collective-permute-done((bf16[1536]{0:T(1024)(128)(2,1)S(1)}, bf16[1536]{0:T(1024)(128)(2,1)S(1)}, u32[]{:S(2)}, u32[]{:S(2)}) %collective-permute-start) | collective-permute-done | bytes 3104 | tf_op jit(solution)/shard_map/ppermute | solution.py:13
  64.1 74.4 %all-gather.6.cloned.1.call-done = bf16[1,1024,1536]{2,1,0:T(8,128)(2,1)} async-done(((bf16[1,128,1536]{2,1,0:T(8,128)(2,1)}), bf16[1,1024,1536]{2,1,0:T(8,128)(2,1)}) %all-gather.6.cloned.1.call-update) | async-done | bytes 3145744 | tf_op jit(solution)/shard_map/all_gather | solution.py:42
  138.5 2.7 fusion.4
  141.3 0.1 copy-done.4
  141.4 4.5 %fusion.18 = f32[1024,768]{1,0:T(8,128)S(1)} fusion(bf16[1,1536,768]{2,1,0:T(8,128)(2,1)} %param.12, bf16[1,1024,1536]{2,1,0:T(8,128)(2,1)S(1)} %copy-done.4, f32[1536]{0:T(1024)S(1)} %convert_reduce_fusion, f32[1024]{0:T(1024)S(1)} %add_rsqrt_fusion), kind=kOutput, calls=%fused_computation.30 | convolution fusion | flops 2422210560 | bytes 8660992 | tf_op jit(solution)/shard_map/dot_general | solution.py:23
  145.9 4.6 %multiply_convert_fusion.3 = (bf16[1024,768]{1,0:T(8,128)(2,1)S(1)}, f32[1024,768]{1,0:T(8,128)}) fusion(f32[1024,768]{1,0:T(8,128)S(1)} %fusion.18, bf16[1,1536,768]{2,1,0:T(8,128)(2,1)S(1)} %copy-done.8, bf16[1,1024,1536]{2,1,0:T(8,128)(2,1)S(1)} %copy-done.4, f32[1536]{0:T(1024)S(1)} %convert_reduce_fusion, f32[1024]{0:T(1024)S(1)} %add_rsqrt_fusion), kind=kOutput, calls=%fused_computation.15 | convolution fusion | flops 2426929152 | bytes 13379584 | tf_op jit(solution)/shard_map/dot_general | solution.py:24
  150.5 4.8 %fusion.11 = f32[1024,1536]{1,0:T(8,128)} fusion(bf16[1024,768]{1,0:T(8,128)(2,1)S(1)} %get-tuple-element.9, bf16[1,768,1536]{2,1,0:T(8,128)(2,1)S(1)} %copy-done), kind=kOutput, calls=%fused_computation.23 | convolution fusion | flops 2415919104 | bytes 10223616 | tf_op jit(solution)/shard_map/dot_general | solution.py:55
  155.3 6.0 %fusion.25 = f32[1024,768]{1,0:T(8,128)} fusion(bf16[1536,768]{1,0:T(8,128)(2,1)} %collective-permute-done.2, bf16[1,1024,1536]{2,1,0:T(8,128)(2,1)S(1)} %copy-done.4, f32[1536]{0:T(1024)S(1)} %convert_element_type.70, f32[1024]{0:T(1024)S(1)} %add_rsqrt_fusion), kind=kOutput, calls=%fused_computation.40 | convolution fusion | flops 2422210560 | bytes 8660992 | tf_op jit(solution)/shard_map/dot_general | solution.py:24
  161.3 13.9 %subtract_convert_fusion = bf16[1024,1536]{1,0:T(8,128)(2,1)} fusion(f32[1024,1536]{1,0:T(8,128)} %fusion.11, bf16[768,1536]{1,0:T(8,128)(2,1)} %collective-permute-done.3, f32[1024,768]{1,0:T(8,128)} %fusion.25, bf16[1536,768]{1,0:T(8,128)(2,1)} %collective-permute-done.1, bf16[1,1024,1536]{2,1,0:T(8,128)(2,1)} %all-gather.6.cloned.1.call-done, ...), kind=kOutput, calls=%fused_computation.8 | convolution fusion | flops 4845993984 | bytes 20457472 | tf_op jit(solution)/shard_map/dot_general | solution.py:56
  175.3 77.3 %reduce-scatter.3.cloned.1.call-done = bf16[128,1536]{1,0:T(8,128)(2,1)} async-done(((bf16[1024,1536]{1,0:T(8,128)(2,1)}), bf16[128,1536]{1,0:T(8,128)(2,1)}) %reduce-scatter.3.cloned.1.call-update) | async-done | bytes 393232 | tf_op jit(solution)/shard_map/reduce_scatter | solution.py:53
  252.6 1.9 fusion.39
  254.6 62.6 %all-gather.4.cloned.1.call-done = bf16[1024,1536]{1,0:T(8,128)(2,1)} async-done(((bf16[128,1536]{1,0:T(8,128)(2,1)}), bf16[1024,1536]{1,0:T(8,128)(2,1)}) %all-gather.4.cloned.1.call-update) | async-done | bytes 3145744 | tf_op jit(solution)/shard_map/all_gather | solution.py:63
  317.1 7.2 %multiply_convert_fusion = (bf16[1024,768]{1,0:T(8,128)(2,1)S(1)}, bf16[1024,768]{1,0:T(8,128)(2,1)S(1)}) fusion(f32[1024,768]{1,0:T(8,128)} %copy-done.14, f32[1024,768]{1,0:T(8,128)} %get-tuple-element.10, bf16[1024,1536]{1,0:T(8,128)(2,1)} %all-gather.4.cloned.1.call-done, bf16[1,768,1536]{2,1,0:T(8,128)(2,1)S(1)} %copy-done), kind=kOutput, calls=%fused_computation.12 | convolution fusion | flops 2426142720 | bytes 14942208 | tf_op jit(solution)/shard_map/rd,fd->rf/dot_general | solution.py:64
  324.3 2.6 fusion.16
  327.0 0.1 copy-done.9
  327.1 4.3 add_convert_fusion
  331.4 1.0 copy-done.2
  332.4 0.2 fusion.38
  332.6 0.4 copy-done.11
  333.0 5.9 %fusion.8 = bf16[1,768,1536]{2,1,0:T(8,128)(2,1)} fusion(bf16[1024,768]{1,0:T(8,128)(2,1)S(1)} %copy-done.11, bf16[1024,1536]{1,0:T(8,128)(2,1)} %all-gather.4.cloned.1.call-done), kind=kOutput, calls=%fused_computation.20 | convolution fusion | flops 2417098752 | bytes 7077888 | tf_op jit(solution)/shard_map/rf,rd->fd/dot_general | solution.py:70
  338.9 4.4 fusion.6
  343.2 4.4 fusion.7
  347.6 61.2 %reduce-scatter.5.cloned.1.call-done = bf16[128,1536]{1,0:T(8,128)(2,1)} async-done(((bf16[1024,1536]{1,0:T(8,128)(2,1)}), bf16[128,1536]{1,0:T(8,128)(2,1)}) %reduce-scatter.5.cloned.1.call-update) | async-done | bytes 393232 | tf_op jit(solution)/shard_map/reduce_scatter | solution.py:83
  408.8 1.4 fusion.37
  410.2 22.2 %psum.7 = f32[1,1536]{1,0:T(1,128)} all-reduce(f32[1,1536]{1,0:T(1,128)S(1)} %broadcast_in_dim.25), channel_id=1, replica_groups=mesh['member'=16,'fsdp'=8] {'fsdp'}, use_global_device_ids=true, to_apply=%region_6.7 | all-reduce | flops 1536 | bytes 12288 | tf_op jit(solution)/shard_map/psum | solution.py:87
  432.4 2.1 fusion.40
  (46 shorter events, 0.4 us)
Async XLA Ops:
  7.2 143.3 %copy-start = (bf16[1,768,1536]{2,1,0:T(8,128)(2,1)S(1)}, bf16[1,768,1536]{2,1,0:T(8,128)(2,1)}, u32[]{:S(2)}) copy-start(bf16[1,768,1536]{2,1,0:T(8,128)(2,1)} %param.14) | copy-start | bytes 7077892
  7.2 131.3 %all-gather.6.cloned.1.call-start = ((), (), s32[]{:S(2)}) async-start(), calls=%async_computation.5 | async-start | bytes 3538944 | tf_op jit(solution)/shard_map/all_gather | solution.py:42
  7.9 244.7 %reduce-scatter.3.cloned.1.call-start = ((), (), s32[]{:S(2)}) async-start(), calls=%async_computation.2 | async-start | bytes 3538944 | tf_op jit(solution)/shard_map/reduce_scatter | solution.py:53
  8.0 153.4 %collective-permute-start.3 = (bf16[768,1536]{1,0:T(8,128)(2,1)}, bf16[768,1536]{1,0:T(8,128)(2,1)}, u32[]{:S(2)}, u32[]{:S(2)}) collective-permute-start(bf16[768,1536]{1,0:T(8,128)(2,1)} %bitcast.68), channel_id=1, source_target_pairs={{0,8},{8,16},{16,24},{24,32},{32,40},{40,48},{48,56},{56,64},{64,7... | collective-permute-start | bytes 7077896 | tf_op jit(solution)/shard_map/ppermute | solution.py:13
  8.0 147.3 %collective-permute-start.2 = (bf16[1536,768]{1,0:T(8,128)(2,1)}, bf16[1536,768]{1,0:T(8,128)(2,1)}, u32[]{:S(2)}, u32[]{:S(2)}) collective-permute-start(bf16[1536,768]{1,0:T(8,128)(2,1)} %bitcast.67), channel_id=1, source_target_pairs={{0,8},{8,16},{16,24},{24,32},{32,40},{40,48},{48,56},{56,64},{64,7... | collective-permute-start | bytes 7077896 | tf_op jit(solution)/shard_map/ppermute | solution.py:13
  10.4 53.7 %collective-permute-start = (bf16[1536]{0:T(1024)(128)(2,1)S(1)}, bf16[1536]{0:T(1024)(128)(2,1)S(1)}, u32[]{:S(2)}, u32[]{:S(2)}) collective-permute-start(bf16[1536]{0:T(1024)(128)(2,1)S(1)} %reduce.1), channel_id=1, source_target_pairs={{0,8},{8,16},{16,24},{24,32},{32,40},{40,48},{48,56},{56,64},{64,7... | collective-permute-start | bytes 9224 | tf_op jit(solution)/shard_map/ppermute | solution.py:13
  10.6 150.7 %collective-permute-start.1 = (bf16[1536,768]{1,0:T(8,128)(2,1)}, bf16[1536,768]{1,0:T(8,128)(2,1)}, u32[]{:S(2)}, u32[]{:S(2)}) collective-permute-start(bf16[1536,768]{1,0:T(8,128)(2,1)} %bitcast.69), channel_id=1, source_target_pairs={{0,8},{8,16},{16,24},{24,32},{32,40},{40,48},{48,56},{56,64},{64,7... | collective-permute-start | bytes 7077896 | tf_op jit(solution)/shard_map/ppermute | solution.py:13
  138.5 2.8 copy-start.4
  141.4 4.5 %copy-start.8 = (bf16[1,1536,768]{2,1,0:T(8,128)(2,1)S(1)}, bf16[1,1536,768]{2,1,0:T(8,128)(2,1)}, u32[]{:S(2)}) copy-start(bf16[1,1536,768]{2,1,0:T(8,128)(2,1)} %param.13) | copy-start | bytes 7077892
  145.9 4.6 %copy-start.14 = (f32[1024,768]{1,0:T(8,128)}, f32[1024,768]{1,0:T(8,128)S(1)}, u32[]{:S(2)}) copy-start(f32[1024,768]{1,0:T(8,128)S(1)} %fusion.18) | copy-start | bytes 9437188
  150.5 4.8 %copy-start.10 = (bf16[1024,768]{1,0:T(8,128)(2,1)}, bf16[1024,768]{1,0:T(8,128)(2,1)S(1)}, u32[]{:S(2)}) copy-start(bf16[1024,768]{1,0:T(8,128)(2,1)S(1)} %get-tuple-element.9) | copy-start | bytes 4718596
  175.2 77.4 %copy-start.6 = (bf16[1,128,1536]{2,1,0:T(8,128)(2,1)S(1)}, bf16[1,128,1536]{2,1,0:T(8,128)(2,1)}, u32[]{:S(2)}) copy-start(bf16[1,128,1536]{2,1,0:T(8,128)(2,1)} %param.11) | copy-start | bytes 1179652
  175.2 141.9 %all-gather.4.cloned.1.call-start = ((), (), s32[]{:S(2)}) async-start(), calls=%async_computation.3 | async-start | bytes 3538944 | tf_op jit(solution)/shard_map/all_gather | solution.py:63
  254.5 154.3 %reduce-scatter.5.cloned.1.call-start = ((), (), s32[]{:S(2)}) async-start(), calls=%async_computation.4 | async-start | bytes 3538944 | tf_op jit(solution)/shard_map/reduce_scatter | solution.py:83
  317.1 7.2 %copy-start.7 = (bf16[1,1536,768]{2,1,0:T(8,128)(2,1)S(1)}, bf16[1,1536,768]{2,1,0:T(8,128)(2,1)}, u32[]{:S(2)}) copy-start(bf16[1,1536,768]{2,1,0:T(8,128)(2,1)} %param.12) | copy-start | bytes 7077892
  324.3 2.7 copy-start.12
  324.3 2.7 copy-start.15
  324.3 2.8 copy-start.9
  331.4 1.0 copy-start.2
  331.4 1.5 copy-start.11
  332.9 5.9 %copy-start.5 = (bf16[1,1024,1536]{2,1,0:T(8,128)(2,1)S(1)}, bf16[1,1024,1536]{2,1,0:T(8,128)(2,1)}, u32[]{:S(2)}) copy-start(bf16[1,1024,1536]{2,1,0:T(8,128)(2,1)} %all-gather.6.cloned.1.call-done) | copy-start | bytes 9437188
  332.9 5.9 %copy-start.13 = (bf16[1024,768]{1,0:T(8,128)(2,1)S(1)}, bf16[1024,768]{1,0:T(8,128)(2,1)}, u32[]{:S(2)}) copy-start(bf16[1024,768]{1,0:T(8,128)(2,1)} %copy-done.12) | copy-start | bytes 4718596
  338.9 4.4 copy-start.16
  343.2 89.2 %copy-start.3 = (bf16[128,1536]{1,0:T(8,128)(2,1)S(1)}, bf16[128,1536]{1,0:T(8,128)(2,1)}, u32[]{:S(2)}) copy-start(bf16[128,1536]{1,0:T(8,128)(2,1)} %fusion.39) | copy-start | bytes 1179652
  343.2 91.3 %copy-start.1 = (bf16[1,768,1536]{2,1,0:T(8,128)(2,1)S(1)}, bf16[1,768,1536]{2,1,0:T(8,128)(2,1)}, u32[]{:S(2)}) copy-start(bf16[1,768,1536]{2,1,0:T(8,128)(2,1)} %param.14) | copy-start | bytes 7077892
Sparse Core Ops, SparseCore 0:
  10.3 128.1 all-gather.5
  175.4 77.2 reduce-scatter.2
  255.5 61.5 all-gather.3
  331.6 77.2 reduce-scatter.4
where the time goes:
time: 441 us
  waiting for transfers between devices  328 us (74%)
  matrix products  62.5 us (14%)
  blocking collectives  22.2 us (5%)
  between operations  13.9 us (3%)
  other arithmetic  9.63 us (2%)
    reduce_scatter x1, waiting for transfers between devices, shards(): lax.psum_scatter((jnp.dot(hidden, own_down, preferred_element_type=jnp.fl...  77.3 us
    all_gather x1, waiting for transfers between devices, shards(): gathered = lax.all_gather(own_rows, 'fsdp', axis=0, tiled=True)  74.4 us
    all_gather x1, waiting for transfers between devices, shards(): grad_rows = lax.all_gather(grad_out, 'fsdp', axis=0, tiled=True)  62.6 us
    reduce_scatter x1, waiting for transfers between devices, shards(): lax.psum_scatter((from_gate + from_up).astype(jnp.bfloat16), 'fsdp', scat...  61.2 us
    ppermute x4, waiting for transfers between devices, shifted(): return lax.ppermute(value, axis, pairs)  51.3 us
    psum x1, blocking collectives, shards(): grad_gain = lax.psum(jnp.sum(grad_inputs * own_normed, axis=0), 'fsdp')  22.2 us
    dot_general x1, matrix products, shards(): jnp.dot(peer_hidden, peer_down, preferred_element_type=jnp.float32)  13.9 us
    dot_general x2, matrix products, project_up(): up_value = jnp.dot(inputs, up_weight, preferred_element_type=jnp.float32)  10.6 us
  transfers between devices with their start and end apart: 8, of which 5 were waited for; matrix products, arithmetic and copies ran while one was open for 9% of the time, Pallas kernels for 0%

commit v1 on v0

v1 whole, which is shorter than its diff:
```python
import functools
import jax
import jax.numpy as jnp
from jax import lax
from jax.experimental import pallas as pl
from jax.experimental.pallas import tpu as pltpu
from jax.sharding import PartitionSpec as P

EPS = 1e-05
AGREE = 1.0
MESH = pl.DeviceIdType.MESH
F32 = jnp.float32
BF16 = jnp.bfloat16
D = 1536
FB = 768
N = 8
ROWS = 128
NB = 4
RB = ROWS // NB
M = N * RB

ORDER = (
    ("E1", 0), ("E2", 0), ("E3", 0), ("E5", 0), ("E1", 1), ("E4", 0), ("E3", 1), ("E6", 0), ("E5", 1),
    ("E2", 1), ("E7", 0), ("E1", 2), ("O1", 0), ("O2", 0), ("E4", 1), ("E6", 1), ("O3", 0), ("E3", 2),
    ("E5", 2), ("P1", 0), ("E7", 1), ("E2", 2), ("E1", 3), ("P2", 0), ("P3", 0), ("E4", 2), ("E6", 2),
    ("P4", 0), ("E3", 3), ("E5", 3), ("O1", 1), ("O2", 1), ("E7", 2), ("E2", 3), ("P1", 1), ("P2", 1),
    ("E4", 3), ("E6", 3), ("P3", 1), ("P4", 1), ("O3", 1), ("E7", 3), ("O1", 2), ("O2", 2), ("F0", 0),
    ("P1", 2), ("P2", 2), ("P3", 2), ("F2", 0), ("F2b", 0), ("P4", 2), ("P1", 3), ("P2", 3), ("F0", 1),
    ("F3", 0), ("P3", 3), ("P4", 3), ("O3", 2), ("F4", 0), ("F2", 1), ("F2b", 1), ("O1", 3), ("O2", 3),
    ("F0", 2), ("G2", 0), ("G3", 0), ("G5", 0), ("O3", 3), ("F3", 1), ("F2", 2), ("F2b", 2), ("F4", 1),
    ("F0", 3), ("G4", 0), ("G3", 1), ("G6", 0), ("F3", 2), ("G5", 1), ("F2b", 3), ("G2", 1), ("F4", 2),
    ("F2", 3), ("G7", 0), ("B1", 0), ("G3", 2), ("B2", 0), ("G4", 1), ("G6", 1), ("B3", 0), ("B4", 0),
    ("G2", 2), ("G5", 2), ("F3", 3), ("G4", 2), ("G6", 2), ("G7", 1), ("B1", 1), ("F4", 3), ("S2", 0),
    ("S2b", 0), ("B2", 1), ("B3", 1), ("B4", 1), ("G3", 3), ("G7", 2), ("B1", 2), ("B2", 2), ("G2", 3),
    ("G5", 3), ("B3", 2), ("S3", 0), ("B4", 2), ("S2", 1), ("S2b", 1), ("S4", 0), ("G4", 3), ("G6", 3),
    ("S2b", 2), ("S2", 2), ("S3", 1), ("G7", 3), ("B1", 3), ("S3", 2), ("B2", 3), ("S4", 1), ("B3", 3),
    ("B4", 3), ("S4", 2), ("K1", 0), ("WD", 0), ("WD", 1), ("S2", 3), ("S2b", 3), ("K2", 0), ("WD", 2),
    ("WG", 0), ("WG", 1), ("WG", 2), ("WG", 3), ("S3", 3), ("WG", 4), ("WG", 5), ("WU", 0), ("WU", 1),
    ("WU", 2), ("WU", 3), ("S4", 3), ("WU", 4), ("WU", 5),
)


def dot_nn(a, b):
    return jnp.dot(a, b, preferred_element_type=F32)


def dot_nt(a, b):
    return lax.dot_general(a, b, (((1,), (1,)), ((), ())), preferred_element_type=F32)


def dot_tn(a, b):
    return lax.dot_general(a, b, (((0,), (0,)), ((), ())), preferred_element_type=F32)


def blocks(total, size, body):
    @pl.loop(0, total // size)
    def _(i):
        body(pl.multiple_of(i * size, size))


def kernel(
    tokens, upstream, gate_w, up_w, down_w, gain, stale_gate, stale_up, stale_down, stale_gain,
    out_tokens, out_gate, out_up, out_down, out_gain,
    wg, wu, wd, sg, su, sd, ups, tok, tok_next, x, xs, inv, gv, uv, gt, ut, hid, hid_s,
    gap, peer, rs1, rs2, go, ggp, gup, outt, acc, acc_in, gain_buf,
    send, recv, local,
):
    member = lax.axis_index("member")
    j = lax.axis_index("fsdp")
    y, z = j // 4, j % 4
    members = lax.axis_size("member")
    z_up, z_dn, z_far = (z + 1) % 4, (z + 3) % 4, (z + 2) % 4
    other = 1 - y
    UP, DN, ACROSS = (member, y * 4 + z_up), (member, y * 4 + z_dn), (member, other * 4 + z)
    NEXT = ((member + 1) % members, j)
    PREV = ((member + members - 1) % members, j)

    pos = {
        "o": j,
        "ou": y * 4 + z_up,
        "od": y * 4 + z_dn,
        "of": y * 4 + z_far,
        "x": other * 4 + z,
        "xu": other * 4 + z_up,
        "xd": other * 4 + z_dn,
        "xf": other * 4 + z_far,
    }

    def rows(b, chunk):
        return pl.ds(pl.multiple_of(b * M + pos[chunk] * RB, 16), RB)

    def batch(b):
        return pl.ds(b * M, M)

    numbers = {}

    def number(key):
        return numbers.setdefault(key, len(numbers))

    def remote(key, src, dst, device):
        i = number(key)
        return pltpu.make_async_remote_copy(
            src_ref=src,
            dst_ref=dst,
            send_sem=send.at[i],
            recv_sem=recv.at[i],
            device_id=device,
            device_id_type=MESH,
        )

    sent = []

    def start(key, src, dst, device):
        copy = remote(key, src, dst, device)
        copy.start()
        sent.append((key, copy))

    def arrive(key, dst, device):
        remote(key, dst, dst, device).wait_recv()

    locals_ = {}

    def fetch(key, src, dst):
        copy = pltpu.make_async_copy(src, dst, local.at[len(locals_)])
        locals_[key] = copy
        copy.start()

    done = set()

    def need(key):
        if key not in done:
            done.add(key)
            locals_[key].wait()

    for b in range(NB):
        fetch(("t", b), tokens.at[0, pl.ds(b * RB, RB)], tok.at[rows(b, "o")])
    fetch("sg", stale_gate.at[0], sg)
    fetch("su", stale_up.at[0], su)
    fetch("sd", stale_down.at[0], sd)
    fetch("wg", gate_w.at[0], wg)
    fetch("wu", up_w.at[0], wu)
    fetch("wd", down_w.at[0], wd)
    fetch("ups", upstream.at[0], ups)

    barrier = pltpu.get_barrier_semaphore()
    for step in range(1, N):
        pl.semaphore_signal(barrier, inc=1, device_id=(member, (j + step) % N), device_id_type=MESH)
    for device in (NEXT, PREV):
        pl.semaphore_signal(barrier, inc=1, device_id=device, device_id_type=MESH)
    pl.semaphore_wait(barrier, N + 1)
    acc[...] = jnp.zeros_like(acc)

    def onward(b, chunk):
        start(("n", b, chunk), tok.at[rows(b, chunk)], tok_next.at[rows(b, chunk)], PREV)

    def gather(name, ref, then):
        def move(b, chunk, way, device):
            start((name, b, chunk, way), ref.at[rows(b, chunk)], ref.at[rows(b, chunk)], device)

        def got(b, chunk, sent_as, way):
            arrive((name, b, sent_as, way), ref.at[rows(b, chunk)], UP)
            then(b, chunk)

        def e1(b):
            if name == "a":
                need(("t", b))
            for way, device in (("u", UP), ("a", ACROSS), ("d", DN)):
                move(b, "o", way, device)
            then(b, "o")

        def e2(b):
            got(b, "od", "o", "u")
            move(b, "od", "u", UP)

        def e3(b):
            got(b, "x", "o", "a")
            move(b, "x", "d", DN)
            move(b, "x", "u", UP)

        def e4(b):
            got(b, "xu", "x", "d")
            move(b, "xu", "d", DN)

        def e5(b):
            got(b, "ou", "o", "d")

        def e6(b):
            got(b, "xd", "x", "u")

        def e7(b):
            got(b, "of", "od", "u")
            got(b, "xf", "xu", "d")

        return e1, e2, e3, e4, e5, e6, e7

    def scatter(name, ref, land, first_key):
        def slot(b, k):
            return land.at[pl.ds((b * 7 + k) * RB, RB)]

        def push(b, chunk, k, device):
            start((name, b, k), ref.at[rows(b, chunk)], slot(b, k), device)

        def landed(b, k):
            arrive((name, b, k), slot(b, k), UP)

        def add(b, chunk, slots):
            r = rows(b, chunk)
            total = ref[r, :].astype(F32)
            for k in slots:
                total = total + slot(b, k)[...].astype(F32)
            return r, total

        def f1(b):
            push(b, "xf", 0, UP)
            push(b, "of", 1, DN)
            push(b, "xd", 3, DN)
            push(b, "ou", 2, UP)

        def f2(b):
            landed(b, 0)
            r, total = add(b, "xu", (0,))
            ref[r, :] = total.astype(BF16)
            push(b, "xu", 4, UP)

        def f2b(b):
            landed(b, 1)
            r, total = add(b, "od", (1,))
            ref[r, :] = total.astype(BF16)
            push(b, "od", 5, DN)

        def f3(b):
            landed(b, 3)
            landed(b, 4)
            r, total = add(b, "x", (3, 4))
            ref[r, :] = total.astype(BF16)
            push(b, "x", 6, ACROSS)

        def f4(b):
            for k in (2, 5, 6):
                landed(b, k)

        def result(b, first, size):
            at = pl.multiple_of(b * M + j * RB + first, 16)
            total = ref[pl.ds(at, size), :].astype(F32)
            for k in (2, 5, 6):
                total = total + land[pl.ds((b * 7 + k) * RB + first, size), :].astype(F32)
            return total

        return f1, f2, f2b, f3, f4, result

    ea = gather("a", tok, onward)
    eg = gather("g", go, lambda b, chunk: None)
    ra = scatter("r", gap, rs1, None)
    rg = scatter("s", peer, rs2, None)

    gain_row = gain[...].astype(F32)
    stale_row = stale_gain[...].astype(F32)

    def normalize(src, dst, at_dst, b, factor, keep):
        def body(at):
            values = src[pl.ds(pl.multiple_of(b * M + at, 16), 16), :].astype(F32)
            scale = lax.rsqrt(jnp.mean(values * values, axis=-1, keepdims=True) + EPS)
            dst[pl.ds(pl.multiple_of(at_dst + at, 16), 16), :] = (values * scale * factor).astype(BF16)
            if keep:
                inv[pl.ds(pl.multiple_of(b * M + at, 16), 16), :] = scale

        blocks(M, 16, body)

    def activate(g_ref, u_ref, base, dst, at_dst):
        def body(at):
            g = g_ref[pl.ds(pl.multiple_of(base + at, 16), 16), :]
            u = u_ref[pl.ds(pl.multiple_of(base + at, 16), 16), :]
            dst[pl.ds(pl.multiple_of(at_dst + at, 16), 16), :] = (g * jax.nn.sigmoid(g) * u).astype(BF16)

        blocks(M, 16, body)

    def p1(b):
        for chunk in pos:
            arrive(("n", b, chunk), tok_next.at[rows(b, chunk)], PREV)
        normalize(tok_next, xs, 0, b, stale_row, False)

    def p2(b):
        need("sg")
        gt[...] = dot_nn(xs[...], sg[...])

    def p3(b):
        need("su")
        ut[...] = dot_nn(xs[...], su[...])
        activate(gt, ut, 0, hid_s, 0)

    def p4(b):
        need("sd")
        peer[batch(b), :] = dot_nn(hid_s[...], sd[...]).astype(BF16)
        start(("p", b), peer.at[batch(b)], gap.at[batch(b)], NEXT)

    def o1(b):
        normalize(tok, x, b * M, b, gain_row, True)

    def o2(b):
        need("wg")
        gv[batch(b), :] = dot_nn(x[batch(b), :], wg[...])

    def o3(b):
        need("wu")
        uv[batch(b), :] = dot_nn(x[batch(b), :], wu[...])
        activate(gv, uv, b * M, hid, b * M)

    def f0(b):
        need("wd")
        arrive(("p", b), gap.at[batch(b)], PREV)
        own = dot_nn(hid[batch(b), :], wd[...])
        gap[batch(b), :] = (own - gap[batch(b), :].astype(F32)).astype(BF16)
        ra[0](b)

    def f4(b):
        need("ups")
        ra[4](b)
        for first in range(0, RB, 16):
            total = ra[5](b, first, 16)
            mine = ups[pl.ds(b * RB + first, 16), :].astype(F32) + AGREE * total
            go[pl.ds(pl.multiple_of(b * M + j * RB + first, 16), 16), :] = mine.astype(BF16)
        eg[0](b)

    def b1(b):
        gt[...] = dot_nt(go[batch(b), :], wd[...])

        def body(at):
            g = gv[pl.ds(pl.multiple_of(b * M + at, 16), 16), :]
            s = jax.nn.sigmoid(g)
            gh = gt[pl.ds(at, 16), :]
            u = uv[pl.ds(pl.multiple_of(b * M + at, 16), 16), :]
            ggp[pl.ds(pl.multiple_of(b * M + at, 16), 16), :] = (gh * u * s * (1.0 + g * (1.0 - s))).astype(BF16)
            gup[pl.ds(pl.multiple_of(b * M + at, 16), 16), :] = (gh * (g * s)).astype(BF16)

        blocks(M, 16, body)

    def back(b, half):
        if half == 0:
            for key, copy in sent:
                if key == ("p", b):
                    copy.wait_send()
            waited.add(("p", b))
        cols = pl.ds(half * FB, FB)
        total = dot_nt(ggp[batch(b), :], wg[cols, :]) + dot_nt(gup[batch(b), :], wu[cols, :])
        peer[batch(b), cols] = total.astype(BF16)

    waited = set()

    def b2(b):
        back(b, 0)

    def b3(b):
        back(b, 1)
        rg[0](b)

    def b4(b):
        def body(at):
            r = pl.ds(pl.multiple_of(b * M + at, 16), 16)
            part = part_of[r, :].astype(F32) * (tok[r, :].astype(F32) * inv[r, :])
            acc[...] += part[:8] + part[8:]

        part_of = peer
        blocks(M, 16, body)

    def k1(b):
        for step in range(1, N):
            start(("k", step), acc, acc_in.at[step], (member, (j + step) % N))

    def k2(b):
        total = acc[...]
        for step in range(1, N):
            arrive(("k", step), acc_in.at[step], (member, (j + step) % N))
            total = total + acc_in[step]
        gain_buf[...] = jnp.sum(total, axis=0, keepdims=True)
        fetch("ok", gain_buf, out_gain)

    def f4g(b):
        rg[4](b)
        for first in range(0, RB, 16):
            grad_in = rg[5](b, first, 16)
            r = pl.ds(pl.multiple_of(b * M + j * RB + first, 16), 16)
            scale = inv[r, :]
            normed = tok[r, :].astype(F32) * scale
            grad_normed = grad_in * gain_row
            mean = jnp.mean(grad_normed * normed, axis=-1, keepdims=True)
            outt[pl.ds(b * RB + first, 16), :] = (
                go[r, :].astype(F32) + scale * (grad_normed - normed * mean)
            ).astype(BF16)
        fetch(("ot", b), outt.at[pl.ds(b * RB, RB)], out_tokens.at[0, pl.ds(b * RB, RB)])

    def weight(name, left, right, dst, out, size):
        def task(i):
            r = pl.ds(i * size, size)
            dst[r, :] = dot_tn(left[:, i * size : (i + 1) * size], right[...]).astype(BF16)
            fetch((name, i), dst.at[r], out.at[0, r])

        return task

    tasks = {
        "P1": p1, "P2": p2, "P3": p3, "P4": p4, "O1": o1, "O2": o2, "O3": o3, "F0": f0, "F4": f4,
        "F2": ra[1], "F2b": ra[2], "F3": ra[3], "S2": rg[1], "S2b": rg[2], "S3": rg[3], "S4": f4g,
        "B1": b1, "B2": b2, "B3": b3, "B4": b4, "K1": k1, "K2": k2,
        "WD": weight("wd", hid, go, sd, out_down, 256),
        "WG": weight("wg", x, ggp, sg, out_gate, 256),
        "WU": weight("wu", x, gup, su, out_up, 256),
    }
    for i in range(7):
        tasks["E%d" % (i + 1)] = ea[i]
        tasks["G%d" % (i + 1)] = eg[i]
    for name, index in ORDER:
        tasks[name](index)

    for key, copy in sent:
        if key not in waited:
            copy.wait_send()
    for key in locals_:
        need(key)


def shards(
    tokens, upstream, gate_weight, up_weight, down_weight, norm_gain,
    stale_gate, stale_up, stale_down, stale_gain,
):
    hbm = pl.BlockSpec(memory_space=pl.ANY)
    vmem = pl.BlockSpec(memory_space=pltpu.VMEM)
    total = N * ROWS
    wide = pltpu.VMEM((total, D), BF16)
    narrow = pltpu.VMEM((total, FB), F32)
    half = pltpu.VMEM((total, FB), BF16)
    tall = pltpu.VMEM((D, FB), BF16)
    flat = pltpu.VMEM((FB, D), BF16)
    step = pltpu.VMEM((M, FB), F32)
    land = pltpu.VMEM((NB * 7 * RB, D), BF16)
    return pl.pallas_call(
        kernel,
        out_shape=(
            jax.ShapeDtypeStruct((1, ROWS, D), BF16),
            jax.ShapeDtypeStruct((1, D, FB), BF16),
            jax.ShapeDtypeStruct((1, D, FB), BF16),
            jax.ShapeDtypeStruct((1, FB, D), BF16),
            jax.ShapeDtypeStruct((1, D), F32),
        ),
        in_specs=[hbm, hbm, hbm, hbm, hbm, vmem, hbm, hbm, hbm, vmem],
        out_specs=(hbm,) * 5,
        scratch_shapes=[
            tall, tall, flat, tall, tall, flat,
            pltpu.VMEM((ROWS, D), BF16),
            wide, wide, wide,
            pltpu.VMEM((M, D), BF16),
            pltpu.VMEM((total, 1), F32),
            narrow, narrow, step, step, half,
            pltpu.VMEM((M, FB), BF16),
            wide, wide, land, land, wide, half, half,
            pltpu.VMEM((ROWS, D), BF16),
            pltpu.VMEM((8, D), F32),
            pltpu.VMEM((N, 8, D), F32),
            pltpu.VMEM((1, D), F32),
            pltpu.SemaphoreType.DMA((NB * 37 + 8,)),
            pltpu.SemaphoreType.DMA((NB * 37 + 8,)),
            pltpu.SemaphoreType.DMA((2 * NB + 7 + 16,)),
        ],
        compiler_params=pltpu.CompilerParams(
            collective_id=0, has_side_effects=True, vmem_limit_bytes=62 * 2**20
        ),
        name="layer",
    )(
        tokens, upstream, gate_weight, up_weight, down_weight, norm_gain,
        stale_gate, stale_up, stale_down, stale_gain,
    )


def solution(mesh):
    in_specs = (
        P("member", "fsdp", None),
        P("member", "fsdp", None),
        P("member", None, "fsdp"),
        P("member", None, "fsdp"),
        P("member", "fsdp", None),
        P("member", None),
        P("member", None, "fsdp"),
        P("member", None, "fsdp"),
        P("member", "fsdp", None),
        P("member", None),
    )
    out_specs = (
        P("member", "fsdp", None),
        P("member", None, "fsdp"),
        P("member", None, "fsdp"),
        P("member", "fsdp", None),
        P("member", None),
    )
    return jax.shard_map(shards, mesh=mesh, in_specs=in_specs, out_specs=out_specs, check_vma=False)
```

time: 441 us -> 190 us (0.43)
  waiting for transfers between devices: 328 us -> 0 us
  Pallas kernels: 0 us -> 179 us
  matrix products: 62.5 us -> 0 us
  blocking collectives: 22.2 us -> 0 us
  between operations: 13.9 us -> 0.65 us
  other arithmetic: 9.63 us -> 0 us
  local copies, waits for them, and re-layouts: 1.64 us -> 9.66 us
    pallas_call x0 -> x1, Pallas kernels: none -> 179 us  [shards(): pl.pallas_call(kernel, out_shape=(jax.ShapeDtypeStruct((1, ROWS, D), BF16...]
    reduce_scatter x2 -> x0, waiting for transfers between devices: 139 us -> none  [the longest x1 77.3 us: shards(): lax.psum_scatter((jnp.dot(hidden, own_down, preferred_element_type=jnp.fl...]
    all_gather x2 -> x0, waiting for transfers between devices: 137 us -> none  [the longest x1 74.4 us: shards(): gathered = lax.all_gather(own_rows, 'fsdp', axis=0, tiled=True)]
    dot_general x11 -> x0, matrix products: 62.5 us -> none  [the longest x1 13.9 us: shards(): jnp.dot(peer_hidden, peer_down, preferred_element_type=jnp.float32)]
    ppermute x4 -> x0, waiting for transfers between devices: 51.3 us -> none  [shifted(): return lax.ppermute(value, axis, pairs)]
    psum x1 -> x0, blocking collectives: 22.2 us -> none  [shards(): grad_gain = lax.psum(jnp.sum(grad_inputs * own_normed, axis=0), 'fsdp')]
    unnamed x34 -> x11, local copies, waits for them, and re-layouts: 1.63 us -> 9.66 us
  transfers between devices with their start and end apart: 8 -> 0, of which waited for: 5 -> 0; matrix products, arithmetic and copies ran while one was open for 9% -> 0% of each run, Pallas kernels for 0% -> 0%
where the time goes in v1:
time: 190 us
  Pallas kernels  179 us (94%)
  local copies, waits for them, and re-layouts  9.66 us (5%)
    pallas_call x1, Pallas kernels, shards(): pl.pallas_call(kernel, out_shape=(jax.ShapeDtypeStruct((1, ROWS, D), BF16...  179 us
    unnamed x11, local copies, waits for them, and re-layouts  9.66 us

profile of v1, /device:TPU:0, one launch (start us, length us, event | category | flops | bytes accessed | tf_op | source)
XLA Modules:
  0.0 189.6 jit_solution(8548882711252859370)
XLA Ops:
  0.6 179.3 %layer.1 = (bf16[1,128,1536]{2,1,0:T(8,128)(2,1)}, bf16[1,1536,768]{2,1,0:T(8,128)(2,1)}, bf16[1,1536,768]{2,1,0:T(8,128)(2,1)}, bf16[1,768,1536]{2,1,0:T(8,128)(2,1)}, f32[1,1536]{1,0:T(1,128)}) custom-call(bf16[1,128,1536]{2,1,0:T(8,128)(2,1)} %tokens.1, bf16[1,128,1536]{2,1,0:T(8,128)(2,1)} %upstream.1, bf16[1,1536,768]{2,1,0:T(8,128)(2,1)} %gate_w.1, ...), custom_call_target="tpu_custom_call" | custom-call | tf_op jit(solution)/shard_map/layer/pallas_call | solution.py:434
  180.0 1.8 copy.20
  181.7 0.0 copy-start.1
  181.7 3.4 %copy.21 = bf16[1,1536,768]{2,1,0:T(8,128)(2,1)} copy(bf16[1,1536,768]{2,1,0:T(8,128)(2,1)} %get-tuple-element.11) | data formatting | bytes 4718592
  185.1 0.0 copy-done.1
  185.1 0.0 copy-start
  185.1 1.4 copy.22
  186.5 1.1 copy-done
  187.6 0.0 copy-start.2
  187.6 1.4 copy.23
  189.0 0.0 copy-done.2
  189.0 0.6 copy.24
Async XLA Ops:
  181.7 3.4 %copy-start.1 = (bf16[1,1536,768]{2,1,0:T(8,128)(2,1)S(1)}, bf16[1,1536,768]{2,1,0:T(8,128)(2,1)}, u32[]{:S(2)}) copy-start(bf16[1,1536,768]{2,1,0:T(8,128)(2,1)} %get-tuple-element.12) | copy-start | bytes 7077892
  185.1 2.5 %copy-start = (bf16[1,768,1536]{2,1,0:T(8,128)(2,1)S(1)}, bf16[1,768,1536]{2,1,0:T(8,128)(2,1)}, u32[]{:S(2)}) copy-start(bf16[1,768,1536]{2,1,0:T(8,128)(2,1)} %get-tuple-element.13) | copy-start | bytes 7077892
  187.6 1.4 copy-start.2

commit v2 on v1

--- a/solution.py
+++ b/solution.py
@@ -20,23 +20,23 @@
 M = N * RB
 
 ORDER = (
-    ("E1", 0), ("E2", 0), ("E3", 0), ("E5", 0), ("E1", 1), ("E4", 0), ("E3", 1), ("E6", 0), ("E5", 1),
-    ("E2", 1), ("E7", 0), ("E1", 2), ("O1", 0), ("O2", 0), ("E4", 1), ("E6", 1), ("O3", 0), ("E3", 2),
-    ("E5", 2), ("P1", 0), ("E7", 1), ("E2", 2), ("E1", 3), ("P2", 0), ("P3", 0), ("E4", 2), ("E6", 2),
-    ("P4", 0), ("E3", 3), ("E5", 3), ("O1", 1), ("O2", 1), ("E7", 2), ("E2", 3), ("P1", 1), ("P2", 1),
-    ("E4", 3), ("E6", 3), ("P3", 1), ("P4", 1), ("O3", 1), ("E7", 3), ("O1", 2), ("O2", 2), ("F0", 0),
-    ("P1", 2), ("P2", 2), ("P3", 2), ("F2", 0), ("F2b", 0), ("P4", 2), ("P1", 3), ("P2", 3), ("F0", 1),
-    ("F3", 0), ("P3", 3), ("P4", 3), ("O3", 2), ("F4", 0), ("F2", 1), ("F2b", 1), ("O1", 3), ("O2", 3),
-    ("F0", 2), ("G2", 0), ("G3", 0), ("G5", 0), ("O3", 3), ("F3", 1), ("F2", 2), ("F2b", 2), ("F4", 1),
-    ("F0", 3), ("G4", 0), ("G3", 1), ("G6", 0), ("F3", 2), ("G5", 1), ("F2b", 3), ("G2", 1), ("F4", 2),
-    ("F2", 3), ("G7", 0), ("B1", 0), ("G3", 2), ("B2", 0), ("G4", 1), ("G6", 1), ("B3", 0), ("B4", 0),
-    ("G2", 2), ("G5", 2), ("F3", 3), ("G4", 2), ("G6", 2), ("G7", 1), ("B1", 1), ("F4", 3), ("S2", 0),
-    ("S2b", 0), ("B2", 1), ("B3", 1), ("B4", 1), ("G3", 3), ("G7", 2), ("B1", 2), ("B2", 2), ("G2", 3),
-    ("G5", 3), ("B3", 2), ("S3", 0), ("B4", 2), ("S2", 1), ("S2b", 1), ("S4", 0), ("G4", 3), ("G6", 3),
-    ("S2b", 2), ("S2", 2), ("S3", 1), ("G7", 3), ("B1", 3), ("S3", 2), ("B2", 3), ("S4", 1), ("B3", 3),
-    ("B4", 3), ("S4", 2), ("K1", 0), ("WD", 0), ("WD", 1), ("S2", 3), ("S2b", 3), ("K2", 0), ("WD", 2),
-    ("WG", 0), ("WG", 1), ("WG", 2), ("WG", 3), ("S3", 3), ("WG", 4), ("WG", 5), ("WU", 0), ("WU", 1),
-    ("WU", 2), ("WU", 3), ("S4", 3), ("WU", 4), ("WU", 5),
+    ("E1", 0), ("E2", 0), ("E1", 2), ("E1", 1), ("E1", 3), ("E5", 0), ("E3", 0), ("E6", 0), ("E4", 0),
+    ("E7", 0), ("O1", 0), ("E5", 1), ("E3", 1), ("E6", 1), ("E2", 1), ("E4", 1), ("P1", 0), ("E3", 2),
+    ("P2", 0), ("E7", 1), ("P3", 0), ("P4", 0), ("E5", 2), ("O2", 0), ("E3", 3), ("E6", 2), ("E2", 2),
+    ("E4", 2), ("E2", 3), ("O1", 1), ("P1", 1), ("P2", 1), ("P3", 1), ("E7", 2), ("P4", 1), ("E5", 3),
+    ("E6", 3), ("O3", 0), ("O1", 2), ("F0", 0), ("E7", 3), ("P1", 2), ("P2", 2), ("O2", 2), ("F2b", 0),
+    ("F2", 0), ("P3", 2), ("E4", 3), ("O2", 1), ("P4", 2), ("O3", 1), ("F0", 1), ("F3", 0), ("P1", 3),
+    ("P2", 3), ("P3", 3), ("P4", 3), ("F4", 0), ("F2", 1), ("O1", 3), ("O3", 2), ("F0", 2), ("G2", 0),
+    ("O2", 3), ("G5", 0), ("F2b", 1), ("O3", 3), ("F0", 3), ("F2", 2), ("F3", 1), ("G3", 0), ("G4", 0),
+    ("F4", 1), ("F2", 3), ("G7", 0), ("F3", 2), ("G6", 0), ("B1", 0), ("B2", 0), ("G2", 1), ("F2b", 2),
+    ("G3", 1), ("B3", 0), ("B4", 0), ("F2b", 3), ("G5", 1), ("F3", 3), ("F4", 2), ("G4", 1), ("F4", 3),
+    ("G2", 2), ("G7", 1), ("G6", 1), ("G3", 2), ("G5", 2), ("B1", 1), ("G2", 3), ("G5", 3), ("G4", 2),
+    ("S2b", 0), ("G3", 3), ("B2", 1), ("B3", 1), ("B4", 1), ("S2", 0), ("G6", 2), ("G4", 3), ("G7", 2),
+    ("B1", 2), ("B2", 2), ("G6", 3), ("B3", 2), ("B4", 2), ("G7", 3), ("S2", 1), ("B1", 3), ("B2", 3),
+    ("B3", 3), ("WG", 1), ("WG", 4), ("S2b", 2), ("WG", 2), ("B4", 3), ("S3", 0), ("S2", 2), ("WU", 1),
+    ("WU", 5), ("WU", 2), ("S2", 3), ("WG", 3), ("K1", 0), ("S3", 1), ("WU", 3), ("WG", 0), ("S2b", 3),
+    ("WG", 5), ("S4", 0), ("S2b", 1), ("S3", 2), ("WD", 0), ("S3", 3), ("WU", 4), ("WD", 1), ("WU", 0),
+    ("WD", 2), ("K2", 0), ("S4", 3), ("S4", 2), ("S4", 1),
 )
 
 
@@ -74,6 +74,9 @@
     UP, DN, ACROSS = (member, y * 4 + z_up), (member, y * 4 + z_dn), (member, other * 4 + z)
     NEXT = ((member + 1) % members, j)
     PREV = ((member + members - 1) % members, j)
+    edge_prev, edge_next = ((member + 7) % 8) // 7, (member % 8) // 7
+    PREV_X = (PREV[0], ((y + edge_prev) % 2) * 4 + z)
+    NEXT_X = (NEXT[0], ((y + edge_next) % 2) * 4 + z)
 
     pos = {
         "o": j,
@@ -132,6 +135,12 @@
             done.add(key)
             locals_[key].wait()
 
+    barrier = pltpu.get_barrier_semaphore()
+    for step in range(1, N):
+        pl.semaphore_signal(barrier, inc=1, device_id=(member, (j + step) % N), device_id_type=MESH)
+    for to in (NEXT[0], PREV[0]):
+        for at in (y, other):
+            pl.semaphore_signal(barrier, inc=1, device_id=(to, at * 4 + z), device_id_type=MESH)
     for b in range(NB):
         fetch(("t", b), tokens.at[0, pl.ds(b * RB, RB)], tok.at[rows(b, "o")])
     fetch("sg", stale_gate.at[0], sg)
@@ -141,117 +150,144 @@
     fetch("wu", up_w.at[0], wu)
     fetch("wd", down_w.at[0], wd)
     fetch("ups", upstream.at[0], ups)
-
-    barrier = pltpu.get_barrier_semaphore()
-    for step in range(1, N):
-        pl.semaphore_signal(barrier, inc=1, device_id=(member, (j + step) % N), device_id_type=MESH)
-    for device in (NEXT, PREV):
-        pl.semaphore_signal(barrier, inc=1, device_id=device, device_id_type=MESH)
-    pl.semaphore_wait(barrier, N + 1)
     acc[...] = jnp.zeros_like(acc)
+    pl.semaphore_wait(barrier, N + 3)
+
+    mirror = {"ou": "od", "od": "ou", "xu": "xd", "xd": "xu"}
+
+    def side(b, chunk):
+        return mirror.get(chunk, chunk) if b % 2 else chunk
+
+    def ways(b):
+        return (DN, UP) if b % 2 else (UP, DN)
 
     def onward(b, chunk):
-        start(("n", b, chunk), tok.at[rows(b, chunk)], tok_next.at[rows(b, chunk)], PREV)
-
-    def gather(name, ref, then):
+        chunk = side(b, chunk)
+        if chunk[0] == "o":
+            start(("n", b, chunk), tok.at[rows(b, chunk)], tok_next.at[rows(b, chunk)], PREV)
+        else:
+            at = ((other + edge_prev) % 2) * 4 + pos[chunk] % 4
+            r = pl.ds(pl.multiple_of(b * M + at * RB, 16), RB)
+            start(("n", b, chunk), tok.at[r], tok_next.at[r], PREV_X)
+
+    def gather(name, ref, then, crossings):
         def move(b, chunk, way, device):
-            start((name, b, chunk, way), ref.at[rows(b, chunk)], ref.at[rows(b, chunk)], device)
+            r = rows(b, side(b, chunk))
+            start((name, b, chunk, way), ref.at[r], ref.at[r], device)
 
         def got(b, chunk, sent_as, way):
-            arrive((name, b, sent_as, way), ref.at[rows(b, chunk)], UP)
-            then(b, chunk)
+            arrive((name, b, sent_as, way), ref.at[rows(b, side(b, chunk))], UP)
 
         def e1(b):
-            if name == "a":
-                need(("t", b))
-            for way, device in (("u", UP), ("a", ACROSS), ("d", DN)):
-                move(b, "o", way, device)
-            then(b, "o")
+            up, dn = ways(b)
+            if name == "g":
+                move(b, "o", "a", ACROSS)
+            elif b == 0:
+                for each in range(NB):
+                    need(("t", each))
+                    move(each, "o", "a", ACROSS)
+                    if each == 0:
+                        move(b, "o", "u", up)
+                        move(b, "o", "d", dn)
+                for each in range(NB):
+                    then(each, "o")
+                return
+            move(b, "o", "u", up)
+            move(b, "o", "d", dn)
 
         def e2(b):
             got(b, "od", "o", "u")
-            move(b, "od", "u", UP)
+            if crossings == 2:
+                move(b, "od", "a", ACROSS)
+            move(b, "od", "u", ways(b)[0])
+            then(b, "od")
 
         def e3(b):
             got(b, "x", "o", "a")
-            move(b, "x", "d", DN)
-            move(b, "x", "u", UP)
+            move(b, "x", "d", ways(b)[1])
+            if crossings == 1:
+                move(b, "x", "u", ways(b)[0])
+            then(b, "x")
 
         def e4(b):
-            got(b, "xu", "x", "d")
-            move(b, "xu", "d", DN)
+            if crossings == 2:
+                got(b, "xd", "od", "a")
+                move(b, "xd", "u", ways(b)[0])
+            else:
+                got(b, "xd", "x", "u")
+            then(b, "xd")
 
         def e5(b):
             got(b, "ou", "o", "d")
+            then(b, "ou")
 
         def e6(b):
-            got(b, "xd", "x", "u")
+            got(b, "xu", "x", "d")
+            if crossings == 1:
+                move(b, "xu", "d", ways(b)[1])
+            then(b, "xu")
 
         def e7(b):
             got(b, "of", "od", "u")
-            got(b, "xf", "xu", "d")
+            if crossings == 2:
+                got(b, "xf", "xd", "u")
+            else:
+                got(b, "xf", "xu", "d")
+            then(b, "of")
+            then(b, "xf")
 
         return e1, e2, e3, e4, e5, e6, e7
 
-    def scatter(name, ref, land, first_key):
+    def scatter(name, ref, land):
         def slot(b, k):
             return land.at[pl.ds((b * 7 + k) * RB, RB)]
 
         def push(b, chunk, k, device):
-            start((name, b, k), ref.at[rows(b, chunk)], slot(b, k), device)
-
-        def landed(b, k):
-            arrive((name, b, k), slot(b, k), UP)
-
-        def add(b, chunk, slots):
-            r = rows(b, chunk)
-            total = ref[r, :].astype(F32)
-            for k in slots:
-                total = total + slot(b, k)[...].astype(F32)
-            return r, total
+            start((name, b, k), ref.at[rows(b, side(b, chunk))], slot(b, k), device)
+
+        def merge(b, chunk, slots, k, device):
+            for each in slots:
+                arrive((name, b, each), slot(b, each), UP)
+            total = ref[rows(b, side(b, chunk)), :].astype(F32)
+            for each in slots:
+                total = total + slot(b, each)[...].astype(F32)
+            at = slot(b, slots[0])
+            at[...] = total.astype(BF16)
+            start((name, b, k), at, slot(b, k), device)
 
         def f1(b):
-            push(b, "xf", 0, UP)
-            push(b, "of", 1, DN)
-            push(b, "xd", 3, DN)
-            push(b, "ou", 2, UP)
+            up, dn = ways(b)
+            push(b, "xf", 0, dn)
+            push(b, "xu", 2, up)
+            push(b, "of", 1, dn)
+            push(b, "ou", 3, up)
 
         def f2(b):
-            landed(b, 0)
-            r, total = add(b, "xu", (0,))
-            ref[r, :] = total.astype(BF16)
-            push(b, "xu", 4, UP)
+            merge(b, "xd", (0,), 4, ACROSS)
 
         def f2b(b):
-            landed(b, 1)
-            r, total = add(b, "od", (1,))
-            ref[r, :] = total.astype(BF16)
-            push(b, "od", 5, DN)
+            merge(b, "x", (2,), 5, ACROSS)
 
         def f3(b):
-            landed(b, 3)
-            landed(b, 4)
-            r, total = add(b, "x", (3, 4))
-            ref[r, :] = total.astype(BF16)
-            push(b, "x", 6, ACROSS)
+            merge(b, "od", (1, 4), 6, ways(b)[1])
 
         def f4(b):
-            for k in (2, 5, 6):
-                landed(b, k)
+            for k in (3, 5, 6):
+                arrive((name, b, k), slot(b, k), UP)
 
         def result(b, first, size):
             at = pl.multiple_of(b * M + j * RB + first, 16)
             total = ref[pl.ds(at, size), :].astype(F32)
-            for k in (2, 5, 6):
+            for k in (3, 5, 6):
                 total = total + land[pl.ds((b * 7 + k) * RB + first, size), :].astype(F32)
             return total
 
         return f1, f2, f2b, f3, f4, result
 
-    ea = gather("a", tok, onward)
-    eg = gather("g", go, lambda b, chunk: None)
-    ra = scatter("r", gap, rs1, None)
-    rg = scatter("s", peer, rs2, None)
+    ea = gather("a", tok, onward, 1)
+    eg = gather("g", go, lambda b, chunk: None, 2)
+    ra = scatter("r", gap, rs1)
+    rg = scatter("s", peer, rs2)
 
     gain_row = gain[...].astype(F32)
     stale_row = stale_gain[...].astype(F32)
@@ -291,7 +327,9 @@
     def p4(b):
         need("sd")
         peer[batch(b), :] = dot_nn(hid_s[...], sd[...]).astype(BF16)
-        start(("p", b), peer.at[batch(b)], gap.at[batch(b)], NEXT)
+        for half, device in ((0, NEXT), (1, NEXT_X)):
+            r = pl.ds(b * M + half * (M // 2), M // 2)
+            start(("p", b, half), peer.at[r], gap.at[r], device)
 
     def o1(b):
         normalize(tok, x, b * M, b, gain_row, True)
@@ -307,7 +345,8 @@
 
     def f0(b):
         need("wd")
-        arrive(("p", b), gap.at[batch(b)], PREV)
+        for half in range(2):
+            arrive(("p", b, half), gap.at[pl.ds(b * M + half * (M // 2), M // 2)], PREV)
         own = dot_nn(hid[batch(b), :], wd[...])
         gap[batch(b), :] = (own - gap[batch(b), :].astype(F32)).astype(BF16)
         ra[0](b)
@@ -337,9 +376,9 @@
     def back(b, half):
         if half == 0:
             for key, copy in sent:
-                if key == ("p", b):
+                if key[:2] == ("p", b):
                     copy.wait_send()
-            waited.add(("p", b))
+                    waited.add(key)
         cols = pl.ds(half * FB, FB)
         total = dot_nt(ggp[batch(b), :], wg[cols, :]) + dot_nt(gup[batch(b), :], wu[cols, :])
         peer[batch(b), cols] = total.astype(BF16)
@@ -415,6 +454,27 @@
             copy.wait_send()
     for key in locals_:
         need(key)
+
+
+def hand_over(*refs):
+    sources, results, holds, sems = refs[:5], refs[5:10], refs[10:15], refs[15]
+    steps = []
+    for i, (src, hold, dst) in enumerate(zip(sources, holds, results)):
+        whole = src.shape[1]
+        parts = 4 if 0 < i < 4 else 1
+        for part in range(parts):
+            r = pl.ds(part * (whole // parts), whole // parts)
+            steps.append((
+                pltpu.make_async_copy(src.at[:, r], hold.at[:, r], sems.at[0, i, part]),
+                pltpu.make_async_copy(hold.at[:, r], dst.at[:, r], sems.at[1, i, part]),
+            ))
+    for first, _ in steps:
+        first.start()
+    for first, second in steps:
+        first.wait()
+        second.start()
+    for _, second in steps:
+        second.wait()
 
 
 def shards(
@@ -431,15 +491,16 @@
     flat = pltpu.VMEM((FB, D), BF16)
     step = pltpu.VMEM((M, FB), F32)
     land = pltpu.VMEM((NB * 7 * RB, D), BF16)
-    return pl.pallas_call(
+    results = (
+        jax.ShapeDtypeStruct((1, ROWS, D), BF16),
+        jax.ShapeDtypeStruct((1, D, FB), BF16),
+        jax.ShapeDtypeStruct((1, D, FB), BF16),
+        jax.ShapeDtypeStruct((1, FB, D), BF16),
+        jax.ShapeDtypeStruct((1, D), F32),
+    )
+    parts = pl.pallas_call(
         kernel,
-        out_shape=(
-            jax.ShapeDtypeStruct((1, ROWS, D), BF16),
-            jax.ShapeDtypeStruct((1, D, FB), BF16),
-            jax.ShapeDtypeStruct((1, D, FB), BF16),
-            jax.ShapeDtypeStruct((1, FB, D), BF16),
-            jax.ShapeDtypeStruct((1, D), F32),
-        ),
+        out_shape=results,
         in_specs=[hbm, hbm, hbm, hbm, hbm, vmem, hbm, hbm, hbm, vmem],
         out_specs=(hbm,) * 5,
         scratch_shapes=[
@@ -455,8 +516,8 @@
             pltpu.VMEM((8, D), F32),
             pltpu.VMEM((N, 8, D), F32),
             pltpu.VMEM((1, D), F32),
-            pltpu.SemaphoreType.DMA((NB * 37 + 8,)),
-            pltpu.SemaphoreType.DMA((NB * 37 + 8,)),
+            pltpu.SemaphoreType.DMA((NB * 38 + 8,)),
+            pltpu.SemaphoreType.DMA((NB * 38 + 8,)),
             pltpu.SemaphoreType.DMA((2 * NB + 7 + 16,)),
         ],
         compiler_params=pltpu.CompilerParams(
@@ -467,6 +528,16 @@
         tokens, upstream, gate_weight, up_weight, down_weight, norm_gain,
         stale_gate, stale_up, stale_down, stale_gain,
     )
+    return pl.pallas_call(
+        hand_over,
+        out_shape=results,
+        in_specs=[hbm] * 5,
+        out_specs=(hbm,) * 5,
+        scratch_shapes=[pltpu.VMEM(r.shape, r.dtype) for r in results]
+        + [pltpu.SemaphoreType.DMA((2, 5, 4))],
+        compiler_params=pltpu.CompilerParams(vmem_limit_bytes=62 * 2**20),
+        name="hand_over",
+    )(*parts)
 
 
 def solution(mesh):

time: 190 us -> 154 us (0.81)
  Pallas kernels: 179 us -> 153 us
  local copies, waits for them, and re-layouts: 9.66 us -> 0 us
    pallas_call x1 -> x2, Pallas kernels: 179 us -> 153 us  [the longest x1 147 us: shards(): pl.pallas_call(kernel, out_shape=results, in_specs=[hbm, hbm, hbm, hbm, h...]
    unnamed x11 -> x0, local copies, waits for them, and re-layouts: 9.66 us -> none
where the time goes in v2:
time: 154 us; the launch traced here: 153 us
  Pallas kernels  153 us (99%)
    pallas_call x1, Pallas kernels, shards(): pl.pallas_call(kernel, out_shape=results, in_specs=[hbm, hbm, hbm, hbm, h...  147 us
    pallas_call x1, Pallas kernels, shards(): pl.pallas_call(hand_over, out_shape=results, in_specs=[hbm] * 5, out_spec...  6.12 us

profile of v2, /device:TPU:0, one launch (start us, length us, event | category | flops | bytes accessed | tf_op | source)
XLA Modules:
  0.0 153.5 jit_solution(2422782921520804644)
XLA Ops:
  0.6 146.5 %layer.1 = (bf16[1,128,1536]{2,1,0:T(8,128)(2,1)}, bf16[1,1536,768]{2,1,0:T(8,128)(2,1)}, bf16[1,1536,768]{2,1,0:T(8,128)(2,1)}, bf16[1,768,1536]{2,1,0:T(8,128)(2,1)}, f32[1,1536]{1,0:T(1,128)}) custom-call(bf16[1,128,1536]{2,1,0:T(8,128)(2,1)} %tokens.1, bf16[1,128,1536]{2,1,0:T(8,128)(2,1)} %upstream.1, bf16[1,1536,768]{2,1,0:T(8,128)(2,1)} %gate_w.1, ...), custom_call_target="tpu_custom_call" | custom-call | tf_op jit(solution)/shard_map/layer/pallas_call | solution.py:501
  147.2 6.1 %hand_over.1 = (bf16[1,128,1536]{2,1,0:T(8,128)(2,1)}, bf16[1,1536,768]{2,1,0:T(8,128)(2,1)}, bf16[1,1536,768]{2,1,0:T(8,128)(2,1)}, bf16[1,768,1536]{2,1,0:T(8,128)(2,1)}, f32[1,1536]{1,0:T(1,128)}) custom-call(bf16[1,128,1536]{2,1,0:T(8,128)(2,1)} %get-tuple-element.10.refs_0_, bf16[1,1536,768]{2,1,0:T(8,128)(2,1)} %get-tuple-element.11.refs_1_, ...), custom_call_target="tpu_custom_call" | custom-call | tf_op jit(solution)/shard_map/hand_over/pallas_call | solution.py:531

commit v3 on v2

--- a/solution.py
+++ b/solution.py
@@ -17,27 +17,10 @@
 ROWS = 128
 NB = 4
 RB = ROWS // NB
+KR, KG, KS = 1, 2, 2
 M = N * RB
 
-ORDER = (
-    ("E1", 0), ("E2", 0), ("E1", 2), ("E1", 1), ("E1", 3), ("E5", 0), ("E3", 0), ("E6", 0), ("E4", 0),
-    ("E7", 0), ("O1", 0), ("E5", 1), ("E3", 1), ("E6", 1), ("E2", 1), ("E4", 1), ("P1", 0), ("E3", 2),
-    ("P2", 0), ("E7", 1), ("P3", 0), ("P4", 0), ("E5", 2), ("O2", 0), ("E3", 3), ("E6", 2), ("E2", 2),
-    ("E4", 2), ("E2", 3), ("O1", 1), ("P1", 1), ("P2", 1), ("P3", 1), ("E7", 2), ("P4", 1), ("E5", 3),
-    ("E6", 3), ("O3", 0), ("O1", 2), ("F0", 0), ("E7", 3), ("P1", 2), ("P2", 2), ("O2", 2), ("F2b", 0),
-    ("F2", 0), ("P3", 2), ("E4", 3), ("O2", 1), ("P4", 2), ("O3", 1), ("F0", 1), ("F3", 0), ("P1", 3),
-    ("P2", 3), ("P3", 3), ("P4", 3), ("F4", 0), ("F2", 1), ("O1", 3), ("O3", 2), ("F0", 2), ("G2", 0),
-    ("O2", 3), ("G5", 0), ("F2b", 1), ("O3", 3), ("F0", 3), ("F2", 2), ("F3", 1), ("G3", 0), ("G4", 0),
-    ("F4", 1), ("F2", 3), ("G7", 0), ("F3", 2), ("G6", 0), ("B1", 0), ("B2", 0), ("G2", 1), ("F2b", 2),
-    ("G3", 1), ("B3", 0), ("B4", 0), ("F2b", 3), ("G5", 1), ("F3", 3), ("F4", 2), ("G4", 1), ("F4", 3),
-    ("G2", 2), ("G7", 1), ("G6", 1), ("G3", 2), ("G5", 2), ("B1", 1), ("G2", 3), ("G5", 3), ("G4", 2),
-    ("S2b", 0), ("G3", 3), ("B2", 1), ("B3", 1), ("B4", 1), ("S2", 0), ("G6", 2), ("G4", 3), ("G7", 2),
-    ("B1", 2), ("B2", 2), ("G6", 3), ("B3", 2), ("B4", 2), ("G7", 3), ("S2", 1), ("B1", 3), ("B2", 3),
-    ("B3", 3), ("WG", 1), ("WG", 4), ("S2b", 2), ("WG", 2), ("B4", 3), ("S3", 0), ("S2", 2), ("WU", 1),
-    ("WU", 5), ("WU", 2), ("S2", 3), ("WG", 3), ("K1", 0), ("S3", 1), ("WU", 3), ("WG", 0), ("S2b", 3),
-    ("WG", 5), ("S4", 0), ("S2b", 1), ("S3", 2), ("WD", 0), ("S3", 3), ("WU", 4), ("WD", 1), ("WU", 0),
-    ("WD", 2), ("K2", 0), ("S4", 3), ("S4", 2), ("S4", 1),
-)
+ORDER = [('E1', 0), ('E1', 1), ('E2', 0), ('E3', 0), ('E5', 0), ('E5', 1), ('N', 1), ('E6', 0), ('E3', 1), ('E4', 0), ('E7', 0), ('E6', 1), ('E1', 2), ('E2', 1), ('E1', 3), ('N', 2), ('E3', 2), ('O1', 0), ('O2', 0), ('E3', 3), ('P1', 0), ('P2', 0), ('E7', 1), ('P3', 0), ('P4', 0), ('E4', 1), ('E2', 2), ('O1', 1), ('E5', 2), ('E6', 2), ('E2', 3), ('O3', 0), ('P1', 1), ('P2', 1), ('E7', 2), ('E4', 2), ('E5', 3), ('E6', 3), ('N', 3), ('P3', 1), ('P4', 1), ('O1', 2), ('E4', 3), ('E7', 3), ('F0', 0), ('P1', 2), ('P2', 2), ('O2', 1), ('P3', 2), ('P4', 2), ('F2b', 0), ('F2', 0), ('O3', 1), ('F0', 1), ('P1', 3), ('P2', 3), ('F3', 0), ('P3', 3), ('O2', 2), ('F2', 1), ('P4', 3), ('F2b', 1), ('O3', 2), ('F0', 2), ('F3', 1), ('F4', 0), ('F2', 2), ('O1', 3), ('F2b', 2), ('O2', 3), ('O3', 3), ('F0', 3), ('F2', 3), ('G2', 0), ('F4', 1), ('F3', 2), ('G4', 0), ('G3', 0), ('G2', 1), ('F3', 3), ('G5', 1), ('G5', 0), ('G3', 1), ('G6', 0), ('G7', 0), ('F4', 2), ('B1', 0), ('F2b', 3), ('G6', 1), ('G4', 1), ('G2', 2), ('F4', 3), ('G7', 1), ('B2', 0), ('G3', 2), ('G4', 2), ('B3', 0), ('G5', 3), ('G2', 3), ('B1', 1), ('G5', 2), ('B2', 1), ('B4', 0), ('G6', 2), ('G7', 2), ('S2', 0), ('G3', 3), ('B1', 2), ('G4', 3), ('B3', 1), ('S2b', 0), ('B4', 1), ('B2', 2), ('G6', 3), ('B3', 2), ('G7', 3), ('B1', 3), ('WG', 0), ('S2', 1), ('S2b', 1), ('WU', 1), ('B2', 3), ('B3', 3), ('WG', 3), ('WG', 4), ('WG', 1), ('S2', 2), ('WG', 5), ('WD', 1), ('WU', 4), ('S2', 3), ('B4', 3), ('S3', 1), ('S2b', 2), ('WU', 0), ('S3', 0), ('B4', 2), ('WU', 2), ('S3', 2), ('K1', 0), ('S3', 3), ('S2b', 3), ('WU', 5), ('WG', 2), ('S4', 1), ('WD', 2), ('WD', 0), ('WU', 3), ('S4', 0), ('S4', 3), ('K2', 0), ('S4', 2)]
 
 
 def dot_nn(a, b):
@@ -62,7 +45,7 @@
     tokens, upstream, gate_w, up_w, down_w, gain, stale_gate, stale_up, stale_down, stale_gain,
     out_tokens, out_gate, out_up, out_down, out_gain,
     wg, wu, wd, sg, su, sd, ups, tok, tok_next, x, xs, inv, gv, uv, gt, ut, hid, hid_s,
-    gap, peer, rs1, rs2, go, ggp, gup, outt, acc, acc_in, gain_buf,
+    gap, peer, rs1, rs2, go, ggp, gup, outt, acc, acc_out, acc_in, gain_buf,
     send, recv, local,
 ):
     member = lax.axis_index("member")
@@ -189,8 +172,7 @@
                     if each == 0:
                         move(b, "o", "u", up)
                         move(b, "o", "d", dn)
-                for each in range(NB):
-                    then(each, "o")
+                then(b, "o")
                 return
             move(b, "o", "u", up)
             move(b, "o", "d", dn)
@@ -238,7 +220,7 @@
 
         return e1, e2, e3, e4, e5, e6, e7
 
-    def scatter(name, ref, land):
+    def scatter(name, ref, land, crossings):
         def slot(b, k):
             return land.at[pl.ds((b * 7 + k) * RB, RB)]
 
@@ -255,39 +237,56 @@
             at[...] = total.astype(BF16)
             start((name, b, k), at, slot(b, k), device)
 
+        last = (3, 5, 6) if crossings == 2 else (2, 5, 6)
+
         def f1(b):
             up, dn = ways(b)
-            push(b, "xf", 0, dn)
-            push(b, "xu", 2, up)
-            push(b, "of", 1, dn)
-            push(b, "ou", 3, up)
+            if crossings == 2:
+                push(b, "xf", 0, dn)
+                push(b, "xu", 2, up)
+                push(b, "of", 1, dn)
+                push(b, "ou", 3, up)
+            else:
+                push(b, "xf", 0, up)
+                push(b, "xd", 3, dn)
+                push(b, "of", 1, dn)
+                push(b, "ou", 2, up)
 
         def f2(b):
-            merge(b, "xd", (0,), 4, ACROSS)
+            if crossings == 2:
+                merge(b, "xd", (0,), 4, ACROSS)
+            else:
+                merge(b, "xu", (0,), 4, ways(b)[0])
 
         def f2b(b):
-            merge(b, "x", (2,), 5, ACROSS)
+            if crossings == 2:
+                merge(b, "x", (2,), 5, ACROSS)
+            else:
+                merge(b, "od", (1,), 5, ways(b)[1])
 
         def f3(b):
-            merge(b, "od", (1, 4), 6, ways(b)[1])
+            if crossings == 2:
+                merge(b, "od", (1, 4), 6, ways(b)[1])
+            else:
+                merge(b, "x", (3, 4), 6, ACROSS)
 
         def f4(b):
-            for k in (3, 5, 6):
+            for k in last:
                 arrive((name, b, k), slot(b, k), UP)
 
         def result(b, first, size):
             at = pl.multiple_of(b * M + j * RB + first, 16)
             total = ref[pl.ds(at, size), :].astype(F32)
-            for k in (3, 5, 6):
+            for k in last:
                 total = total + land[pl.ds((b * 7 + k) * RB + first, size), :].astype(F32)
             return total
 
         return f1, f2, f2b, f3, f4, result
 
     ea = gather("a", tok, onward, 1)
-    eg = gather("g", go, lambda b, chunk: None, 2)
-    ra = scatter("r", gap, rs1)
-    rg = scatter("s", peer, rs2)
+    eg = gather("g", go, lambda b, chunk: None, KG)
+    ra = scatter("r", gap, rs1, KR)
+    rg = scatter("s", peer, rs2, KS)
 
     gain_row = gain[...].astype(F32)
     stale_row = stale_gain[...].astype(F32)
@@ -402,15 +401,16 @@
         blocks(M, 16, body)
 
     def k1(b):
+        acc_out[...] = jnp.sum(acc[...], axis=0, keepdims=True)
         for step in range(1, N):
-            start(("k", step), acc, acc_in.at[step], (member, (j + step) % N))
+            start(("k", step), acc_out, acc_in.at[step], (member, (j + step) % N))
 
     def k2(b):
-        total = acc[...]
+        total = acc_out[...]
         for step in range(1, N):
             arrive(("k", step), acc_in.at[step], (member, (j + step) % N))
             total = total + acc_in[step]
-        gain_buf[...] = jnp.sum(total, axis=0, keepdims=True)
+        gain_buf[...] = total
         fetch("ok", gain_buf, out_gain)
 
     def f4g(b):
@@ -435,7 +435,11 @@
 
         return task
 
+    def n1(b):
+        onward(b, "o")
+
     tasks = {
+        "N": n1,
         "P1": p1, "P2": p2, "P3": p3, "P4": p4, "O1": o1, "O2": o2, "O3": o3, "F0": f0, "F4": f4,
         "F2": ra[1], "F2b": ra[2], "F3": ra[3], "S2": rg[1], "S2b": rg[2], "S3": rg[3], "S4": f4g,
         "B1": b1, "B2": b2, "B3": b3, "B4": b4, "K1": k1, "K2": k2,
@@ -514,7 +518,8 @@
             wide, wide, land, land, wide, half, half,
             pltpu.VMEM((ROWS, D), BF16),
             pltpu.VMEM((8, D), F32),
-            pltpu.VMEM((N, 8, D), F32),
+            pltpu.VMEM((1, D), F32),
+            pltpu.VMEM((N, 1, D), F32),
             pltpu.VMEM((1, D), F32),
             pltpu.SemaphoreType.DMA((NB * 38 + 8,)),
             pltpu.SemaphoreType.DMA((NB * 38 + 8,)),

time: 154 us -> 141 us (0.916)
  Pallas kernels: 153 us -> 140 us
    pallas_call x1, Pallas kernels: 147 us -> 134 us  [shards(): pl.pallas_call(kernel, out_shape=results, in_specs=[hbm, hbm, hbm, hbm, h...]
where the time goes in v3:
time: 141 us
  Pallas kernels  140 us (99%)
    pallas_call x1, Pallas kernels, shards(): pl.pallas_call(kernel, out_shape=results, in_specs=[hbm, hbm, hbm, hbm, h...  134 us
    pallas_call x1, Pallas kernels, shards(): pl.pallas_call(hand_over, out_shape=results, in_specs=[hbm] * 5, out_spec...  6.12 us

profile of v3, /device:TPU:0, one launch (start us, length us, event | category | flops | bytes accessed | tf_op | source)
XLA Modules:
  0.0 140.7 jit_solution(16702950057353192131)
XLA Ops:
  0.6 133.8 %layer.1 = (bf16[1,128,1536]{2,1,0:T(8,128)(2,1)}, bf16[1,1536,768]{2,1,0:T(8,128)(2,1)}, bf16[1,1536,768]{2,1,0:T(8,128)(2,1)}, bf16[1,768,1536]{2,1,0:T(8,128)(2,1)}, f32[1,1536]{1,0:T(1,128)}) custom-call(bf16[1,128,1536]{2,1,0:T(8,128)(2,1)} %tokens.1, bf16[1,128,1536]{2,1,0:T(8,128)(2,1)} %upstream.1, bf16[1,1536,768]{2,1,0:T(8,128)(2,1)} %gate_w.1, ...), custom_call_target="tpu_custom_call" | custom-call | tf_op jit(solution)/shard_map/layer/pallas_call | solution.py:505
  134.4 6.1 %hand_over.1 = (bf16[1,128,1536]{2,1,0:T(8,128)(2,1)}, bf16[1,1536,768]{2,1,0:T(8,128)(2,1)}, bf16[1,1536,768]{2,1,0:T(8,128)(2,1)}, bf16[1,768,1536]{2,1,0:T(8,128)(2,1)}, f32[1,1536]{1,0:T(1,128)}) custom-call(bf16[1,128,1536]{2,1,0:T(8,128)(2,1)} %get-tuple-element.10.refs_0_, bf16[1,1536,768]{2,1,0:T(8,128)(2,1)} %get-tuple-element.11.refs_1_, ...), custom_call_target="tpu_custom_call" | custom-call | tf_op jit(solution)/shard_map/hand_over/pallas_call | solution.py:536

commit v4 on v3

--- a/solution.py
+++ b/solution.py
@@ -20,7 +20,7 @@
 KR, KG, KS = 1, 2, 2
 M = N * RB
 
-ORDER = [('E1', 0), ('E1', 1), ('E2', 0), ('E3', 0), ('E5', 0), ('E5', 1), ('N', 1), ('E6', 0), ('E3', 1), ('E4', 0), ('E7', 0), ('E6', 1), ('E1', 2), ('E2', 1), ('E1', 3), ('N', 2), ('E3', 2), ('O1', 0), ('O2', 0), ('E3', 3), ('P1', 0), ('P2', 0), ('E7', 1), ('P3', 0), ('P4', 0), ('E4', 1), ('E2', 2), ('O1', 1), ('E5', 2), ('E6', 2), ('E2', 3), ('O3', 0), ('P1', 1), ('P2', 1), ('E7', 2), ('E4', 2), ('E5', 3), ('E6', 3), ('N', 3), ('P3', 1), ('P4', 1), ('O1', 2), ('E4', 3), ('E7', 3), ('F0', 0), ('P1', 2), ('P2', 2), ('O2', 1), ('P3', 2), ('P4', 2), ('F2b', 0), ('F2', 0), ('O3', 1), ('F0', 1), ('P1', 3), ('P2', 3), ('F3', 0), ('P3', 3), ('O2', 2), ('F2', 1), ('P4', 3), ('F2b', 1), ('O3', 2), ('F0', 2), ('F3', 1), ('F4', 0), ('F2', 2), ('O1', 3), ('F2b', 2), ('O2', 3), ('O3', 3), ('F0', 3), ('F2', 3), ('G2', 0), ('F4', 1), ('F3', 2), ('G4', 0), ('G3', 0), ('G2', 1), ('F3', 3), ('G5', 1), ('G5', 0), ('G3', 1), ('G6', 0), ('G7', 0), ('F4', 2), ('B1', 0), ('F2b', 3), ('G6', 1), ('G4', 1), ('G2', 2), ('F4', 3), ('G7', 1), ('B2', 0), ('G3', 2), ('G4', 2), ('B3', 0), ('G5', 3), ('G2', 3), ('B1', 1), ('G5', 2), ('B2', 1), ('B4', 0), ('G6', 2), ('G7', 2), ('S2', 0), ('G3', 3), ('B1', 2), ('G4', 3), ('B3', 1), ('S2b', 0), ('B4', 1), ('B2', 2), ('G6', 3), ('B3', 2), ('G7', 3), ('B1', 3), ('WG', 0), ('S2', 1), ('S2b', 1), ('WU', 1), ('B2', 3), ('B3', 3), ('WG', 3), ('WG', 4), ('WG', 1), ('S2', 2), ('WG', 5), ('WD', 1), ('WU', 4), ('S2', 3), ('B4', 3), ('S3', 1), ('S2b', 2), ('WU', 0), ('S3', 0), ('B4', 2), ('WU', 2), ('S3', 2), ('K1', 0), ('S3', 3), ('S2b', 3), ('WU', 5), ('WG', 2), ('S4', 1), ('WD', 2), ('WD', 0), ('WU', 3), ('S4', 0), ('S4', 3), ('K2', 0), ('S4', 2)]
+ORDER = [('E1', 0), ('E1', 2), ('E3', 0), ('E2', 0), ('E1', 1), ('E5', 0), ('E6', 0), ('E3', 1), ('E4', 0), ('E2', 1), ('E7', 0), ('O1', 0), ('E5', 1), ('E6', 1), ('E3', 2), ('E4', 1), ('E1', 3), ('N', 1), ('E3', 3), ('P1', 0), ('P2', 0), ('P4', 0), ('E7', 1), ('N', 2), ('E2', 2), ('E5', 2), ('E4', 2), ('E6', 2), ('O1', 1), ('O2', 0), ('P1', 1), ('P2', 1), ('E2', 3), ('P4', 1), ('E7', 2), ('E5', 3), ('E4', 3), ('N', 3), ('E6', 3), ('O2', 1), ('F0', 0), ('P1', 2), ('P2', 2), ('P4', 2), ('E7', 3), ('F2', 0), ('F0', 1), ('O1', 2), ('O2', 2), ('F2b', 0), ('F3', 0), ('F2', 1), ('P1', 3), ('P2', 3), ('F0', 2), ('P4', 3), ('F2', 2), ('F4', 0), ('O1', 3), ('F2b', 2), ('F2b', 1), ('O2', 3), ('F3', 2), ('F3', 1), ('F0', 3), ('F2', 3), ('G2', 0), ('G5', 0), ('F4', 2), ('F2b', 3), ('F4', 1), ('G3', 0), ('F3', 3), ('G2', 1), ('G4', 0), ('G3', 2), ('G3', 1), ('G6', 0), ('G2', 2), ('F4', 3), ('G7', 0), ('G5', 2), ('G4', 1), ('G5', 1), ('G6', 2), ('B1', 0), ('G2', 3), ('G4', 2), ('B2', 0), ('G6', 1), ('G7', 1), ('G4', 3), ('B1', 1), ('G3', 3), ('S2', 0), ('G7', 2), ('B2', 1), ('G5', 3), ('B1', 2), ('S2b', 0), ('B2', 2), ('G7', 3), ('S2b', 1), ('G6', 3), ('B1', 3), ('S2', 1), ('S3', 0), ('WD', 1), ('B2', 3), ('S2', 2), ('B4', 3), ('S2b', 2), ('WU', 0), ('WU', 1), ('S2', 3), ('S3', 1), ('S3', 2), ('WU', 2), ('S2b', 3), ('WD', 2), ('S4', 0), ('WU', 3), ('S4', 1), ('S3', 3), ('WD', 0), ('S4', 2), ('K1', 0), ('WU', 4), ('WU', 5), ('S4', 3), ('K2', 0)]
 
 
 def dot_nn(a, b):
@@ -44,8 +44,8 @@
 def kernel(
     tokens, upstream, gate_w, up_w, down_w, gain, stale_gate, stale_up, stale_down, stale_gain,
     out_tokens, out_gate, out_up, out_down, out_gain,
-    wg, wu, wd, sg, su, sd, ups, tok, tok_next, x, xs, inv, gv, uv, gt, ut, hid, hid_s,
-    gap, peer, rs1, rs2, go, ggp, gup, outt, acc, acc_out, acc_in, gain_buf,
+    wgu, wd, sgu, sd, ups, tok, tok_next, x, xs, inv, guv, gut, hid, hid_s,
+    gap, peer, rs1, rs2, go, gp, outt, acc, acc_out, acc_in, gain_buf,
     send, recv, local,
 ):
     member = lax.axis_index("member")
@@ -126,11 +126,12 @@
             pl.semaphore_signal(barrier, inc=1, device_id=(to, at * 4 + z), device_id_type=MESH)
     for b in range(NB):
         fetch(("t", b), tokens.at[0, pl.ds(b * RB, RB)], tok.at[rows(b, "o")])
-    fetch("sg", stale_gate.at[0], sg)
-    fetch("su", stale_up.at[0], su)
+    left, right = pl.ds(0, FB), pl.ds(FB, FB)
+    fetch("sg", stale_gate.at[0], sgu.at[:, left])
+    fetch("su", stale_up.at[0], sgu.at[:, right])
     fetch("sd", stale_down.at[0], sd)
-    fetch("wg", gate_w.at[0], wg)
-    fetch("wu", up_w.at[0], wu)
+    fetch("wg", gate_w.at[0], wgu.at[:, left])
+    fetch("wu", up_w.at[0], wgu.at[:, right])
     fetch("wd", down_w.at[0], wd)
     fetch("ups", upstream.at[0], ups)
     acc[...] = jnp.zeros_like(acc)
@@ -301,10 +302,10 @@
 
         blocks(M, 16, body)
 
-    def activate(g_ref, u_ref, base, dst, at_dst):
+    def activate(ref, base, dst, at_dst):
         def body(at):
-            g = g_ref[pl.ds(pl.multiple_of(base + at, 16), 16), :]
-            u = u_ref[pl.ds(pl.multiple_of(base + at, 16), 16), :]
+            r = pl.ds(pl.multiple_of(base + at, 16), 16)
+            g, u = ref[r, left], ref[r, right]
             dst[pl.ds(pl.multiple_of(at_dst + at, 16), 16), :] = (g * jax.nn.sigmoid(g) * u).astype(BF16)
 
         blocks(M, 16, body)
@@ -316,12 +317,9 @@
 
     def p2(b):
         need("sg")
-        gt[...] = dot_nn(xs[...], sg[...])
-
-    def p3(b):
         need("su")
-        ut[...] = dot_nn(xs[...], su[...])
-        activate(gt, ut, 0, hid_s, 0)
+        gut[...] = dot_nn(xs[...], sgu[...])
+        activate(gut, 0, hid_s, 0)
 
     def p4(b):
         need("sd")
@@ -335,12 +333,9 @@
 
     def o2(b):
         need("wg")
-        gv[batch(b), :] = dot_nn(x[batch(b), :], wg[...])
-
-    def o3(b):
         need("wu")
-        uv[batch(b), :] = dot_nn(x[batch(b), :], wu[...])
-        activate(gv, uv, b * M, hid, b * M)
+        guv[batch(b), :] = dot_nn(x[batch(b), :], wgu[...])
+        activate(guv, b * M, hid, b * M)
 
     def f0(b):
         need("wd")
@@ -360,44 +355,34 @@
         eg[0](b)
 
     def b1(b):
-        gt[...] = dot_nt(go[batch(b), :], wd[...])
+        gut[:, left] = dot_nt(go[batch(b), :], wd[...])
 
         def body(at):
-            g = gv[pl.ds(pl.multiple_of(b * M + at, 16), 16), :]
+            r = pl.ds(pl.multiple_of(b * M + at, 16), 16)
+            g, u = guv[r, left], guv[r, right]
             s = jax.nn.sigmoid(g)
-            gh = gt[pl.ds(at, 16), :]
-            u = uv[pl.ds(pl.multiple_of(b * M + at, 16), 16), :]
-            ggp[pl.ds(pl.multiple_of(b * M + at, 16), 16), :] = (gh * u * s * (1.0 + g * (1.0 - s))).astype(BF16)
-            gup[pl.ds(pl.multiple_of(b * M + at, 16), 16), :] = (gh * (g * s)).astype(BF16)
+            gh = gut[pl.ds(at, 16), left]
+            gp[r, left] = (gh * u * s * (1.0 + g * (1.0 - s))).astype(BF16)
+            gp[r, right] = (gh * (g * s)).astype(BF16)
 
         blocks(M, 16, body)
 
-    def back(b, half):
-        if half == 0:
-            for key, copy in sent:
-                if key[:2] == ("p", b):
-                    copy.wait_send()
-                    waited.add(key)
-        cols = pl.ds(half * FB, FB)
-        total = dot_nt(ggp[batch(b), :], wg[cols, :]) + dot_nt(gup[batch(b), :], wu[cols, :])
-        peer[batch(b), cols] = total.astype(BF16)
-
     waited = set()
 
     def b2(b):
-        back(b, 0)
-
-    def b3(b):
-        back(b, 1)
+        for key, copy in sent:
+            if key[:2] == ("p", b):
+                copy.wait_send()
+                waited.add(key)
+        peer[batch(b), :] = dot_nt(gp[batch(b), :], wgu[...]).astype(BF16)
         rg[0](b)
 
     def b4(b):
         def body(at):
             r = pl.ds(pl.multiple_of(b * M + at, 16), 16)
-            part = part_of[r, :].astype(F32) * (tok[r, :].astype(F32) * inv[r, :])
+            part = peer[r, :].astype(F32) * (tok[r, :].astype(F32) * inv[r, :])
             acc[...] += part[:8] + part[8:]
 
-        part_of = peer
         blocks(M, 16, body)
 
     def k1(b):
@@ -422,30 +407,33 @@
             normed = tok[r, :].astype(F32) * scale
             grad_normed = grad_in * gain_row
             mean = jnp.mean(grad_normed * normed, axis=-1, keepdims=True)
+            if b < NB - 1:
+                part = grad_in * normed
+                acc[...] += part[:8] + part[8:]
             outt[pl.ds(b * RB + first, 16), :] = (
                 go[r, :].astype(F32) + scale * (grad_normed - normed * mean)
             ).astype(BF16)
         fetch(("ot", b), outt.at[pl.ds(b * RB, RB)], out_tokens.at[0, pl.ds(b * RB, RB)])
 
-    def weight(name, left, right, dst, out, size):
-        def task(i):
-            r = pl.ds(i * size, size)
-            dst[r, :] = dot_tn(left[:, i * size : (i + 1) * size], right[...]).astype(BF16)
-            fetch((name, i), dst.at[r], out.at[0, r])
-
-        return task
+    def weight_down(i):
+        r = pl.ds(i * 256, 256)
+        sd[r, :] = dot_tn(hid[:, i * 256 : (i + 1) * 256], go[...]).astype(BF16)
+        fetch(("d", i), sd.at[r], out_down.at[0, r])
+
+    def weight_up(i):
+        r = pl.ds(i * 256, 256)
+        sgu[r, :] = dot_tn(x[:, i * 256 : (i + 1) * 256], gp[...]).astype(BF16)
+        fetch(("g", i), sgu.at[r, left], out_gate.at[0, r])
+        fetch(("u", i), sgu.at[r, right], out_up.at[0, r])
 
     def n1(b):
         onward(b, "o")
 
     tasks = {
         "N": n1,
-        "P1": p1, "P2": p2, "P3": p3, "P4": p4, "O1": o1, "O2": o2, "O3": o3, "F0": f0, "F4": f4,
+        "P1": p1, "P2": p2, "P4": p4, "O1": o1, "O2": o2, "F0": f0, "F4": f4,
         "F2": ra[1], "F2b": ra[2], "F3": ra[3], "S2": rg[1], "S2b": rg[2], "S3": rg[3], "S4": f4g,
-        "B1": b1, "B2": b2, "B3": b3, "B4": b4, "K1": k1, "K2": k2,
-        "WD": weight("wd", hid, go, sd, out_down, 256),
-        "WG": weight("wg", x, ggp, sg, out_gate, 256),
-        "WU": weight("wu", x, gup, su, out_up, 256),
+        "B1": b1, "B2": b2, "B4": b4, "K1": k1, "K2": k2, "WD": weight_down, "WU": weight_up,
     }
     for i in range(7):
         tasks["E%d" % (i + 1)] = ea[i]
@@ -489,11 +477,9 @@
     vmem = pl.BlockSpec(memory_space=pltpu.VMEM)
     total = N * ROWS
     wide = pltpu.VMEM((total, D), BF16)
-    narrow = pltpu.VMEM((total, FB), F32)
     half = pltpu.VMEM((total, FB), BF16)
-    tall = pltpu.VMEM((D, FB), BF16)
+    square = pltpu.VMEM((D, D), BF16)
     flat = pltpu.VMEM((FB, D), BF16)
-    step = pltpu.VMEM((M, FB), F32)
     land = pltpu.VMEM((NB * 7 * RB, D), BF16)
     results = (
         jax.ShapeDtypeStruct((1, ROWS, D), BF16),
@@ -508,14 +494,14 @@
         in_specs=[hbm, hbm, hbm, hbm, hbm, vmem, hbm, hbm, hbm, vmem],
         out_specs=(hbm,) * 5,
         scratch_shapes=[
-            tall, tall, flat, tall, tall, flat,
+            square, flat, square, flat,
             pltpu.VMEM((ROWS, D), BF16),
             wide, wide, wide,
             pltpu.VMEM((M, D), BF16),
             pltpu.VMEM((total, 1), F32),
-            narrow, narrow, step, step, half,
+            pltpu.VMEM((total, D), F32), pltpu.VMEM((M, D), F32), half,
             pltpu.VMEM((M, FB), BF16),
-            wide, wide, land, land, wide, half, half,
+            wide, wide, land, land, wide, wide,
             pltpu.VMEM((ROWS, D), BF16),
             pltpu.VMEM((8, D), F32),
             pltpu.VMEM((1, D), F32),

time: 141 us -> 140 us (level)
  no operation moved by 1% of the time
where the time goes in v4:
time: 140 us; the launch traced here: 139 us
  Pallas kernels  139 us (99%)
    pallas_call x1, Pallas kernels, shards(): pl.pallas_call(kernel, out_shape=results, in_specs=[hbm, hbm, hbm, hbm, h...  132 us
    pallas_call x1, Pallas kernels, shards(): pl.pallas_call(hand_over, out_shape=results, in_specs=[hbm] * 5, out_spec...  6.12 us

profile of v4, /device:TPU:0, one launch (start us, length us, event | category | flops | bytes accessed | tf_op | source)
XLA Modules:
  0.0 139.3 jit_solution(10475807724206541779)
XLA Ops:
  0.6 132.4 %layer.1 = (bf16[1,128,1536]{2,1,0:T(8,128)(2,1)}, bf16[1,1536,768]{2,1,0:T(8,128)(2,1)}, bf16[1,1536,768]{2,1,0:T(8,128)(2,1)}, bf16[1,768,1536]{2,1,0:T(8,128)(2,1)}, f32[1,1536]{1,0:T(1,128)}) custom-call(bf16[1,128,1536]{2,1,0:T(8,128)(2,1)} %tokens.1, bf16[1,128,1536]{2,1,0:T(8,128)(2,1)} %upstream.1, bf16[1,1536,768]{2,1,0:T(8,128)(2,1)} %gate_w.1, ...), custom_call_target="tpu_custom_call" | custom-call | tf_op jit(solution)/shard_map/layer/pallas_call | solution.py:491
  133.0 6.1 %hand_over.1 = (bf16[1,128,1536]{2,1,0:T(8,128)(2,1)}, bf16[1,1536,768]{2,1,0:T(8,128)(2,1)}, bf16[1,1536,768]{2,1,0:T(8,128)(2,1)}, bf16[1,768,1536]{2,1,0:T(8,128)(2,1)}, f32[1,1536]{1,0:T(1,128)}) custom-call(bf16[1,128,1536]{2,1,0:T(8,128)(2,1)} %get-tuple-element.10.refs_0_, bf16[1,1536,768]{2,1,0:T(8,128)(2,1)} %get-tuple-element.11.refs_1_, ...), custom_call_target="tpu_custom_call" | custom-call | tf_op jit(solution)/shard_map/hand_over/pallas_call | solution.py:522

commit v5 on v4

--- a/solution.py
+++ b/solution.py
@@ -15,12 +15,33 @@
 FB = 768
 N = 8
 ROWS = 128
-NB = 4
-RB = ROWS // NB
-KR, KG, KS = 1, 2, 2
-M = N * RB
-
-ORDER = [('E1', 0), ('E1', 2), ('E3', 0), ('E2', 0), ('E1', 1), ('E5', 0), ('E6', 0), ('E3', 1), ('E4', 0), ('E2', 1), ('E7', 0), ('O1', 0), ('E5', 1), ('E6', 1), ('E3', 2), ('E4', 1), ('E1', 3), ('N', 1), ('E3', 3), ('P1', 0), ('P2', 0), ('P4', 0), ('E7', 1), ('N', 2), ('E2', 2), ('E5', 2), ('E4', 2), ('E6', 2), ('O1', 1), ('O2', 0), ('P1', 1), ('P2', 1), ('E2', 3), ('P4', 1), ('E7', 2), ('E5', 3), ('E4', 3), ('N', 3), ('E6', 3), ('O2', 1), ('F0', 0), ('P1', 2), ('P2', 2), ('P4', 2), ('E7', 3), ('F2', 0), ('F0', 1), ('O1', 2), ('O2', 2), ('F2b', 0), ('F3', 0), ('F2', 1), ('P1', 3), ('P2', 3), ('F0', 2), ('P4', 3), ('F2', 2), ('F4', 0), ('O1', 3), ('F2b', 2), ('F2b', 1), ('O2', 3), ('F3', 2), ('F3', 1), ('F0', 3), ('F2', 3), ('G2', 0), ('G5', 0), ('F4', 2), ('F2b', 3), ('F4', 1), ('G3', 0), ('F3', 3), ('G2', 1), ('G4', 0), ('G3', 2), ('G3', 1), ('G6', 0), ('G2', 2), ('F4', 3), ('G7', 0), ('G5', 2), ('G4', 1), ('G5', 1), ('G6', 2), ('B1', 0), ('G2', 3), ('G4', 2), ('B2', 0), ('G6', 1), ('G7', 1), ('G4', 3), ('B1', 1), ('G3', 3), ('S2', 0), ('G7', 2), ('B2', 1), ('G5', 3), ('B1', 2), ('S2b', 0), ('B2', 2), ('G7', 3), ('S2b', 1), ('G6', 3), ('B1', 3), ('S2', 1), ('S3', 0), ('WD', 1), ('B2', 3), ('S2', 2), ('B4', 3), ('S2b', 2), ('WU', 0), ('WU', 1), ('S2', 3), ('S3', 1), ('S3', 2), ('WU', 2), ('S2b', 3), ('WD', 2), ('S4', 0), ('WU', 3), ('S4', 1), ('S3', 3), ('WD', 0), ('S4', 2), ('K1', 0), ('WU', 4), ('WU', 5), ('S4', 3), ('K2', 0)]
+RB = (16, 16, 32, 32, 32)
+NB = len(RB)
+FIRST = tuple(sum(RB[:b]) for b in range(NB))
+CROSS = {"a": (1,) * 5, "r": (1, 1, 1, 1, 2), "g": (1, 1, 2, 2, 2), "s": (2,) * 5}
+M = tuple(N * size for size in RB)
+BASE = tuple(N * first for first in FIRST)
+
+ORDER = (
+    ("E1", 0), ("N", 1), ("E1", 2), ("N", 2), ("E1", 1), ("E5", 0), ("E3", 0), ("E3", 1), ("E5", 2),
+    ("E2", 1), ("E5", 1), ("E2", 0), ("E6", 0), ("E4", 0), ("E3", 2), ("E1", 3), ("E7", 0), ("E6", 1),
+    ("O1", 0), ("O2", 0), ("E6", 2), ("E2", 2), ("P1", 0), ("E1", 4), ("E4", 1), ("E7", 1), ("P2", 0),
+    ("P4", 0), ("E4", 2), ("E7", 2), ("E3", 3), ("O1", 1), ("E5", 3), ("E2", 3), ("P1", 1), ("P2", 1),
+    ("P4", 1), ("E6", 3), ("E4", 3), ("E3", 4), ("E2", 4), ("P1", 2), ("P2", 2), ("E7", 3), ("P4", 2),
+    ("N", 3), ("E5", 4), ("N", 4), ("F0", 0), ("O2", 1), ("F0", 1), ("E6", 4), ("O1", 2), ("F2", 1),
+    ("F2", 0), ("F2b", 0), ("E4", 4), ("P1", 3), ("P2", 3), ("P4", 3), ("E7", 4), ("F3", 1), ("F2b", 1),
+    ("F3", 0), ("O2", 2), ("F0", 2), ("O1", 3), ("P1", 4), ("F2", 2), ("P2", 4), ("F2b", 2), ("F4", 1),
+    ("O2", 3), ("F4", 0), ("F3", 2), ("F0", 3), ("P4", 4), ("O1", 4), ("G3", 1), ("O2", 4), ("F4", 2),
+    ("G3", 0), ("G5", 1), ("F2", 3), ("G2", 1), ("G2", 0), ("G2", 2), ("F2b", 3), ("G5", 0), ("G6", 0),
+    ("G6", 1), ("G4", 1), ("F0", 4), ("G7", 0), ("G4", 0), ("F3", 3), ("B1", 0), ("G3", 2), ("B2", 0),
+    ("G7", 1), ("F2", 4), ("F2b", 4), ("B1", 1), ("F4", 3), ("G4", 2), ("F3", 4), ("G5", 2), ("S2", 0),
+    ("B2", 1), ("G2", 3), ("S2b", 0), ("G6", 2), ("G3", 3), ("G7", 2), ("B1", 2), ("F4", 4), ("G4", 3),
+    ("B2", 2), ("G5", 4), ("G3", 4), ("G2", 4), ("S2", 1), ("S3", 0), ("G5", 3), ("S2b", 1), ("G6", 3),
+    ("G7", 3), ("S2b", 2), ("B1", 3), ("G4", 4), ("S2", 2), ("B2", 3), ("S3", 1), ("G6", 4), ("G7", 4),
+    ("B1", 4), ("B2", 4), ("S2", 3), ("S2b", 3), ("WD", 2), ("S3", 2), ("B4", 4), ("S4", 1), ("WU", 4),
+    ("S2", 4), ("S3", 3), ("WD", 0), ("WU", 2), ("S2b", 4), ("WD", 1), ("S4", 0), ("S4", 2), ("S4", 3),
+    ("S3", 4), ("K1", 0), ("WU", 3), ("WU", 0), ("WU", 5), ("WU", 1), ("S4", 4), ("K2", 0),
+)
 
 
 def dot_nn(a, b):
@@ -73,10 +94,10 @@
     }
 
     def rows(b, chunk):
-        return pl.ds(pl.multiple_of(b * M + pos[chunk] * RB, 16), RB)
+        return pl.ds(pl.multiple_of(BASE[b] + pos[chunk] * RB[b], 16), RB[b])
 
     def batch(b):
-        return pl.ds(b * M, M)
+        return pl.ds(BASE[b], M[b])
 
     numbers = {}
 
@@ -125,7 +146,7 @@
         for at in (y, other):
             pl.semaphore_signal(barrier, inc=1, device_id=(to, at * 4 + z), device_id_type=MESH)
     for b in range(NB):
-        fetch(("t", b), tokens.at[0, pl.ds(b * RB, RB)], tok.at[rows(b, "o")])
+        fetch(("t", b), tokens.at[0, pl.ds(FIRST[b], RB[b])], tok.at[rows(b, "o")])
     left, right = pl.ds(0, FB), pl.ds(FB, FB)
     fetch("sg", stale_gate.at[0], sgu.at[:, left])
     fetch("su", stale_up.at[0], sgu.at[:, right])
@@ -151,7 +172,7 @@
             start(("n", b, chunk), tok.at[rows(b, chunk)], tok_next.at[rows(b, chunk)], PREV)
         else:
             at = ((other + edge_prev) % 2) * 4 + pos[chunk] % 4
-            r = pl.ds(pl.multiple_of(b * M + at * RB, 16), RB)
+            r = pl.ds(pl.multiple_of(BASE[b] + at * RB[b], 16), RB[b])
             start(("n", b, chunk), tok.at[r], tok_next.at[r], PREV_X)
 
     def gather(name, ref, then, crossings):
@@ -180,7 +201,7 @@
 
         def e2(b):
             got(b, "od", "o", "u")
-            if crossings == 2:
+            if crossings[b] == 2:
                 move(b, "od", "a", ACROSS)
             move(b, "od", "u", ways(b)[0])
             then(b, "od")
@@ -188,12 +209,12 @@
         def e3(b):
             got(b, "x", "o", "a")
             move(b, "x", "d", ways(b)[1])
-            if crossings == 1:
+            if crossings[b] == 1:
                 move(b, "x", "u", ways(b)[0])
             then(b, "x")
 
         def e4(b):
-            if crossings == 2:
+            if crossings[b] == 2:
                 got(b, "xd", "od", "a")
                 move(b, "xd", "u", ways(b)[0])
             else:
@@ -206,13 +227,13 @@
 
         def e6(b):
             got(b, "xu", "x", "d")
-            if crossings == 1:
+            if crossings[b] == 1:
                 move(b, "xu", "d", ways(b)[1])
             then(b, "xu")
 
         def e7(b):
             got(b, "of", "od", "u")
-            if crossings == 2:
+            if crossings[b] == 2:
                 got(b, "xf", "xd", "u")
             else:
                 got(b, "xf", "xu", "d")
@@ -223,7 +244,7 @@
 
     def scatter(name, ref, land, crossings):
         def slot(b, k):
-            return land.at[pl.ds((b * 7 + k) * RB, RB)]
+            return land.at[pl.ds(7 * FIRST[b] + k * RB[b], RB[b])]
 
         def push(b, chunk, k, device):
             start((name, b, k), ref.at[rows(b, side(b, chunk))], slot(b, k), device)
@@ -238,11 +259,12 @@
             at[...] = total.astype(BF16)
             start((name, b, k), at, slot(b, k), device)
 
-        last = (3, 5, 6) if crossings == 2 else (2, 5, 6)
+        def last(b):
+            return (3, 5, 6) if crossings[b] == 2 else (2, 5, 6)
 
         def f1(b):
             up, dn = ways(b)
-            if crossings == 2:
+            if crossings[b] == 2:
                 push(b, "xf", 0, dn)
                 push(b, "xu", 2, up)
                 push(b, "of", 1, dn)
@@ -254,61 +276,61 @@
                 push(b, "ou", 2, up)
 
         def f2(b):
-            if crossings == 2:
+            if crossings[b] == 2:
                 merge(b, "xd", (0,), 4, ACROSS)
             else:
                 merge(b, "xu", (0,), 4, ways(b)[0])
 
         def f2b(b):
-            if crossings == 2:
+            if crossings[b] == 2:
                 merge(b, "x", (2,), 5, ACROSS)
             else:
                 merge(b, "od", (1,), 5, ways(b)[1])
 
         def f3(b):
-            if crossings == 2:
+            if crossings[b] == 2:
                 merge(b, "od", (1, 4), 6, ways(b)[1])
             else:
                 merge(b, "x", (3, 4), 6, ACROSS)
 
         def f4(b):
-            for k in last:
+            for k in last(b):
                 arrive((name, b, k), slot(b, k), UP)
 
         def result(b, first, size):
-            at = pl.multiple_of(b * M + j * RB + first, 16)
+            at = pl.multiple_of(BASE[b] + j * RB[b] + first, 16)
             total = ref[pl.ds(at, size), :].astype(F32)
-            for k in last:
-                total = total + land[pl.ds((b * 7 + k) * RB + first, size), :].astype(F32)
+            for k in last(b):
+                total = total + land[pl.ds(7 * FIRST[b] + k * RB[b] + first, size), :].astype(F32)
             return total
 
         return f1, f2, f2b, f3, f4, result
 
-    ea = gather("a", tok, onward, 1)
-    eg = gather("g", go, lambda b, chunk: None, KG)
-    ra = scatter("r", gap, rs1, KR)
-    rg = scatter("s", peer, rs2, KS)
+    ea = gather("a", tok, onward, CROSS["a"])
+    eg = gather("g", go, lambda b, chunk: None, CROSS["g"])
+    ra = scatter("r", gap, rs1, CROSS["r"])
+    rg = scatter("s", peer, rs2, CROSS["s"])
 
     gain_row = gain[...].astype(F32)
     stale_row = stale_gain[...].astype(F32)
 
     def normalize(src, dst, at_dst, b, factor, keep):
         def body(at):
-            values = src[pl.ds(pl.multiple_of(b * M + at, 16), 16), :].astype(F32)
+            values = src[pl.ds(pl.multiple_of(BASE[b] + at, 16), 16), :].astype(F32)
             scale = lax.rsqrt(jnp.mean(values * values, axis=-1, keepdims=True) + EPS)
             dst[pl.ds(pl.multiple_of(at_dst + at, 16), 16), :] = (values * scale * factor).astype(BF16)
             if keep:
-                inv[pl.ds(pl.multiple_of(b * M + at, 16), 16), :] = scale
-
-        blocks(M, 16, body)
-
-    def activate(ref, base, dst, at_dst):
+                inv[pl.ds(pl.multiple_of(BASE[b] + at, 16), 16), :] = scale
+
+        blocks(M[b], 16, body)
+
+    def activate(b, ref, base, dst, at_dst):
         def body(at):
             r = pl.ds(pl.multiple_of(base + at, 16), 16)
             g, u = ref[r, left], ref[r, right]
             dst[pl.ds(pl.multiple_of(at_dst + at, 16), 16), :] = (g * jax.nn.sigmoid(g) * u).astype(BF16)
 
-        blocks(M, 16, body)
+        blocks(M[b], 16, body)
 
     def p1(b):
         for chunk in pos:
@@ -318,29 +340,30 @@
     def p2(b):
         need("sg")
         need("su")
-        gut[...] = dot_nn(xs[...], sgu[...])
-        activate(gut, 0, hid_s, 0)
+        own = pl.ds(0, M[b])
+        gut[own, :] = dot_nn(xs[own, :], sgu[...])
+        activate(b, gut, 0, hid_s, 0)
 
     def p4(b):
         need("sd")
-        peer[batch(b), :] = dot_nn(hid_s[...], sd[...]).astype(BF16)
+        peer[batch(b), :] = dot_nn(hid_s[pl.ds(0, M[b]), :], sd[...]).astype(BF16)
         for half, device in ((0, NEXT), (1, NEXT_X)):
-            r = pl.ds(b * M + half * (M // 2), M // 2)
+            r = pl.ds(BASE[b] + half * (M[b] // 2), M[b] // 2)
             start(("p", b, half), peer.at[r], gap.at[r], device)
 
     def o1(b):
-        normalize(tok, x, b * M, b, gain_row, True)
+        normalize(tok, x, BASE[b], b, gain_row, True)
 
     def o2(b):
         need("wg")
         need("wu")
         guv[batch(b), :] = dot_nn(x[batch(b), :], wgu[...])
-        activate(guv, b * M, hid, b * M)
+        activate(b, guv, BASE[b], hid, BASE[b])
 
     def f0(b):
         need("wd")
         for half in range(2):
-            arrive(("p", b, half), gap.at[pl.ds(b * M + half * (M // 2), M // 2)], PREV)
+            arrive(("p", b, half), gap.at[pl.ds(BASE[b] + half * (M[b] // 2), M[b] // 2)], PREV)
         own = dot_nn(hid[batch(b), :], wd[...])
         gap[batch(b), :] = (own - gap[batch(b), :].astype(F32)).astype(BF16)
         ra[0](b)
@@ -348,24 +371,24 @@
     def f4(b):
         need("ups")
         ra[4](b)
-        for first in range(0, RB, 16):
+        for first in range(0, RB[b], 16):
             total = ra[5](b, first, 16)
-            mine = ups[pl.ds(b * RB + first, 16), :].astype(F32) + AGREE * total
-            go[pl.ds(pl.multiple_of(b * M + j * RB + first, 16), 16), :] = mine.astype(BF16)
+            mine = ups[pl.ds(FIRST[b] + first, 16), :].astype(F32) + AGREE * total
+            go[pl.ds(pl.multiple_of(BASE[b] + j * RB[b] + first, 16), 16), :] = mine.astype(BF16)
         eg[0](b)
 
     def b1(b):
-        gut[:, left] = dot_nt(go[batch(b), :], wd[...])
+        gut[pl.ds(0, M[b]), left] = dot_nt(go[batch(b), :], wd[...])
 
         def body(at):
-            r = pl.ds(pl.multiple_of(b * M + at, 16), 16)
+            r = pl.ds(pl.multiple_of(BASE[b] + at, 16), 16)
             g, u = guv[r, left], guv[r, right]
             s = jax.nn.sigmoid(g)
             gh = gut[pl.ds(at, 16), left]
             gp[r, left] = (gh * u * s * (1.0 + g * (1.0 - s))).astype(BF16)
             gp[r, right] = (gh * (g * s)).astype(BF16)
 
-        blocks(M, 16, body)
+        blocks(M[b], 16, body)
 
     waited = set()
 
@@ -379,11 +402,11 @@
 
     def b4(b):
         def body(at):
-            r = pl.ds(pl.multiple_of(b * M + at, 16), 16)
+            r = pl.ds(pl.multiple_of(BASE[b] + at, 16), 16)
             part = peer[r, :].astype(F32) * (tok[r, :].astype(F32) * inv[r, :])
             acc[...] += part[:8] + part[8:]
 
-        blocks(M, 16, body)
+        blocks(M[b], 16, body)
 
     def k1(b):
         acc_out[...] = jnp.sum(acc[...], axis=0, keepdims=True)
@@ -400,9 +423,9 @@
 
     def f4g(b):
         rg[4](b)
-        for first in range(0, RB, 16):
+        for first in range(0, RB[b], 16):
             grad_in = rg[5](b, first, 16)
-            r = pl.ds(pl.multiple_of(b * M + j * RB + first, 16), 16)
+            r = pl.ds(pl.multiple_of(BASE[b] + j * RB[b] + first, 16), 16)
             scale = inv[r, :]
             normed = tok[r, :].astype(F32) * scale
             grad_normed = grad_in * gain_row
@@ -410,10 +433,11 @@
             if b < NB - 1:
                 part = grad_in * normed
                 acc[...] += part[:8] + part[8:]
-            outt[pl.ds(b * RB + first, 16), :] = (
+            outt[pl.ds(FIRST[b] + first, 16), :] = (
                 go[r, :].astype(F32) + scale * (grad_normed - normed * mean)
             ).astype(BF16)
-        fetch(("ot", b), outt.at[pl.ds(b * RB, RB)], out_tokens.at[0, pl.ds(b * RB, RB)])
+        r = pl.ds(FIRST[b], RB[b])
+        fetch(("ot", b), outt.at[r], out_tokens.at[0, r])
 
     def weight_down(i):
         r = pl.ds(i * 256, 256)
@@ -480,7 +504,7 @@
     half = pltpu.VMEM((total, FB), BF16)
     square = pltpu.VMEM((D, D), BF16)
     flat = pltpu.VMEM((FB, D), BF16)
-    land = pltpu.VMEM((NB * 7 * RB, D), BF16)
+    land = pltpu.VMEM((7 * ROWS, D), BF16)
     results = (
         jax.ShapeDtypeStruct((1, ROWS, D), BF16),
         jax.ShapeDtypeStruct((1, D, FB), BF16),
@@ -497,10 +521,10 @@
             square, flat, square, flat,
             pltpu.VMEM((ROWS, D), BF16),
             wide, wide, wide,
-            pltpu.VMEM((M, D), BF16),
+            pltpu.VMEM((max(M), D), BF16),
             pltpu.VMEM((total, 1), F32),
-            pltpu.VMEM((total, D), F32), pltpu.VMEM((M, D), F32), half,
-            pltpu.VMEM((M, FB), BF16),
+            pltpu.VMEM((total, D), F32), pltpu.VMEM((max(M), D), F32), half,
+            pltpu.VMEM((max(M), FB), BF16),
             wide, wide, land, land, wide, wide,
             pltpu.VMEM((ROWS, D), BF16),
             pltpu.VMEM((8, D), F32),

time: 140 us -> 137 us (0.979)
  Pallas kernels: 139 us -> 136 us
    pallas_call x1, Pallas kernels: 132 us -> 130 us  [shards(): pl.pallas_call(kernel, out_shape=results, in_specs=[hbm, hbm, hbm, hbm, h...]
where the time goes in v5:
time: 137 us
  Pallas kernels  136 us (99%)
    pallas_call x1, Pallas kernels, shards(): pl.pallas_call(kernel, out_shape=results, in_specs=[hbm, hbm, hbm, hbm, h...  130 us
    pallas_call x1, Pallas kernels, shards(): pl.pallas_call(hand_over, out_shape=results, in_specs=[hbm] * 5, out_spec...  6.12 us

profile of v5, /device:TPU:0, one launch (start us, length us, event | category | flops | bytes accessed | tf_op | source)
XLA Modules:
  0.0 136.6 jit_solution(4829540841111440839)
XLA Ops:
  0.6 129.6 %layer.1 = (bf16[1,128,1536]{2,1,0:T(8,128)(2,1)}, bf16[1,1536,768]{2,1,0:T(8,128)(2,1)}, bf16[1,1536,768]{2,1,0:T(8,128)(2,1)}, bf16[1,768,1536]{2,1,0:T(8,128)(2,1)}, f32[1,1536]{1,0:T(1,128)}) custom-call(bf16[1,128,1536]{2,1,0:T(8,128)(2,1)} %tokens.1, bf16[1,128,1536]{2,1,0:T(8,128)(2,1)} %upstream.1, bf16[1,1536,768]{2,1,0:T(8,128)(2,1)} %gate_w.1, ...), custom_call_target="tpu_custom_call" | custom-call | tf_op jit(solution)/shard_map/layer/pallas_call | solution.py:515
  130.3 6.1 %hand_over.1 = (bf16[1,128,1536]{2,1,0:T(8,128)(2,1)}, bf16[1,1536,768]{2,1,0:T(8,128)(2,1)}, bf16[1,1536,768]{2,1,0:T(8,128)(2,1)}, bf16[1,768,1536]{2,1,0:T(8,128)(2,1)}, f32[1,1536]{1,0:T(1,128)}) custom-call(bf16[1,128,1536]{2,1,0:T(8,128)(2,1)} %get-tuple-element.10.refs_0_, bf16[1,1536,768]{2,1,0:T(8,128)(2,1)} %get-tuple-element.11.refs_1_, ...), custom_call_target="tpu_custom_call" | custom-call | tf_op jit(solution)/shard_map/hand_over/pallas_call | solution.py:546

commit v6 on v5

--- a/solution.py
+++ b/solution.py
@@ -18,29 +18,29 @@
 RB = (16, 16, 32, 32, 32)
 NB = len(RB)
 FIRST = tuple(sum(RB[:b]) for b in range(NB))
-CROSS = {"a": (1,) * 5, "r": (1, 1, 1, 1, 2), "g": (1, 1, 2, 2, 2), "s": (2,) * 5}
+CROSS = {"a": (1,) * 5, "r": (1, 1, 1, 1, 1), "g": (1, 1, 2, 2, 2), "s": (2,) * 5}
 M = tuple(N * size for size in RB)
 BASE = tuple(N * first for first in FIRST)
 
 ORDER = (
-    ("E1", 0), ("N", 1), ("E1", 2), ("N", 2), ("E1", 1), ("E5", 0), ("E3", 0), ("E3", 1), ("E5", 2),
-    ("E2", 1), ("E5", 1), ("E2", 0), ("E6", 0), ("E4", 0), ("E3", 2), ("E1", 3), ("E7", 0), ("E6", 1),
-    ("O1", 0), ("O2", 0), ("E6", 2), ("E2", 2), ("P1", 0), ("E1", 4), ("E4", 1), ("E7", 1), ("P2", 0),
-    ("P4", 0), ("E4", 2), ("E7", 2), ("E3", 3), ("O1", 1), ("E5", 3), ("E2", 3), ("P1", 1), ("P2", 1),
-    ("P4", 1), ("E6", 3), ("E4", 3), ("E3", 4), ("E2", 4), ("P1", 2), ("P2", 2), ("E7", 3), ("P4", 2),
-    ("N", 3), ("E5", 4), ("N", 4), ("F0", 0), ("O2", 1), ("F0", 1), ("E6", 4), ("O1", 2), ("F2", 1),
-    ("F2", 0), ("F2b", 0), ("E4", 4), ("P1", 3), ("P2", 3), ("P4", 3), ("E7", 4), ("F3", 1), ("F2b", 1),
-    ("F3", 0), ("O2", 2), ("F0", 2), ("O1", 3), ("P1", 4), ("F2", 2), ("P2", 4), ("F2b", 2), ("F4", 1),
-    ("O2", 3), ("F4", 0), ("F3", 2), ("F0", 3), ("P4", 4), ("O1", 4), ("G3", 1), ("O2", 4), ("F4", 2),
-    ("G3", 0), ("G5", 1), ("F2", 3), ("G2", 1), ("G2", 0), ("G2", 2), ("F2b", 3), ("G5", 0), ("G6", 0),
-    ("G6", 1), ("G4", 1), ("F0", 4), ("G7", 0), ("G4", 0), ("F3", 3), ("B1", 0), ("G3", 2), ("B2", 0),
-    ("G7", 1), ("F2", 4), ("F2b", 4), ("B1", 1), ("F4", 3), ("G4", 2), ("F3", 4), ("G5", 2), ("S2", 0),
-    ("B2", 1), ("G2", 3), ("S2b", 0), ("G6", 2), ("G3", 3), ("G7", 2), ("B1", 2), ("F4", 4), ("G4", 3),
-    ("B2", 2), ("G5", 4), ("G3", 4), ("G2", 4), ("S2", 1), ("S3", 0), ("G5", 3), ("S2b", 1), ("G6", 3),
-    ("G7", 3), ("S2b", 2), ("B1", 3), ("G4", 4), ("S2", 2), ("B2", 3), ("S3", 1), ("G6", 4), ("G7", 4),
-    ("B1", 4), ("B2", 4), ("S2", 3), ("S2b", 3), ("WD", 2), ("S3", 2), ("B4", 4), ("S4", 1), ("WU", 4),
-    ("S2", 4), ("S3", 3), ("WD", 0), ("WU", 2), ("S2b", 4), ("WD", 1), ("S4", 0), ("S4", 2), ("S4", 3),
-    ("S3", 4), ("K1", 0), ("WU", 3), ("WU", 0), ("WU", 5), ("WU", 1), ("S4", 4), ("K2", 0),
+    ("E1", 0), ("N", 2), ("E1", 1), ("N", 1), ("E1", 2), ("E3", 0), ("E2", 0), ("E5", 1), ("E3", 1),
+    ("E2", 2), ("E4", 0), ("E5", 0), ("E6", 0), ("E3", 2), ("E7", 0), ("E5", 2), ("E2", 1), ("O1", 0),
+    ("E6", 1), ("O2", 0), ("E6", 2), ("P1", 0), ("E1", 3), ("E1", 4), ("E4", 1), ("P2", 0), ("E7", 1),
+    ("P4", 0), ("O1", 1), ("E4", 2), ("E7", 2), ("P1", 1), ("E3", 3), ("P2", 1), ("P4", 1), ("E2", 3),
+    ("P1", 2), ("E5", 3), ("E6", 3), ("N", 4), ("N", 3), ("P2", 2), ("F0", 0), ("P4", 2), ("O2", 1),
+    ("E3", 4), ("E4", 3), ("E7", 3), ("F2", 0), ("F0", 1), ("O1", 2), ("O2", 2), ("F2", 1), ("P1", 3),
+    ("F3", 0), ("E5", 4), ("P2", 3), ("F2b", 1), ("E6", 4), ("F3", 1), ("P4", 3), ("E2", 4), ("E4", 4),
+    ("F0", 2), ("O1", 3), ("F2b", 0), ("E7", 4), ("O2", 3), ("F2", 2), ("P1", 4), ("F4", 0), ("F4", 1),
+    ("F2b", 2), ("P2", 4), ("P4", 4), ("G2", 0), ("F3", 2), ("F0", 3), ("G3", 0), ("G3", 1), ("G2", 1),
+    ("F2b", 3), ("G5", 0), ("O1", 4), ("F2", 3), ("G6", 0), ("G5", 1), ("G4", 1), ("G6", 1), ("F4", 2),
+    ("O2", 4), ("F0", 4), ("G4", 0), ("G7", 0), ("B1", 0), ("F3", 3), ("F2", 4), ("B2", 0), ("G2", 2),
+    ("F3", 4), ("G7", 1), ("F2b", 4), ("G3", 2), ("F4", 3), ("G4", 2), ("B1", 1), ("F4", 4), ("G5", 2),
+    ("G3", 3), ("G2", 3), ("B2", 1), ("G6", 2), ("S2b", 0), ("G7", 2), ("B1", 2), ("G2", 4), ("G5", 3),
+    ("S2", 0), ("G4", 3), ("G6", 3), ("G5", 4), ("B2", 2), ("S2", 1), ("G7", 3), ("B1", 3), ("S2b", 2),
+    ("G3", 4), ("S2", 2), ("G4", 4), ("S3", 0), ("B2", 3), ("S3", 1), ("S2b", 1), ("G6", 4), ("G7", 4),
+    ("B1", 4), ("B2", 4), ("S2", 3), ("WU", 4), ("WU", 2), ("S4", 0), ("S2b", 3), ("WD", 1), ("WD", 0),
+    ("S3", 3), ("S4", 1), ("S3", 2), ("S2", 4), ("WU", 0), ("WD", 2), ("S2b", 4), ("B4", 4), ("S4", 3),
+    ("S4", 2), ("K1", 0), ("S3", 4), ("WU", 1), ("WU", 5), ("WU", 3), ("S4", 4), ("K2", 0),
 )
 
 
@@ -484,11 +484,14 @@
                 pltpu.make_async_copy(src.at[:, r], hold.at[:, r], sems.at[0, i, part]),
                 pltpu.make_async_copy(hold.at[:, r], dst.at[:, r], sems.at[1, i, part]),
             ))
-    for first, _ in steps:
+    ahead = 5
+    for first, _ in steps[:ahead]:
         first.start()
-    for first, second in steps:
+    for i, (first, second) in enumerate(steps):
         first.wait()
         second.start()
+        if i + ahead < len(steps):
+            steps[i + ahead][0].start()
     for _, second in steps:
         second.wait()
 

time: 137 us -> 142 us (1.036)
  Pallas kernels: 136 us -> 141 us
    pallas_call x1, Pallas kernels: 130 us -> 135 us  [shards(): pl.pallas_call(kernel, out_shape=results, in_specs=[hbm, hbm, hbm, hbm, h...]
where the time goes in v6:
time: 142 us
  Pallas kernels  141 us (99%)
    pallas_call x1, Pallas kernels, shards(): pl.pallas_call(kernel, out_shape=results, in_specs=[hbm, hbm, hbm, hbm, h...  135 us
    pallas_call x1, Pallas kernels, shards(): pl.pallas_call(hand_over, out_shape=results, in_specs=[hbm] * 5, out_spec...  6.76 us

profile of v6, /device:TPU:0, one launch (start us, length us, event | category | flops | bytes accessed | tf_op | source)
XLA Modules:
  0.0 142.1 jit_solution(3659801803358728092)
XLA Ops:
  0.6 134.5 %layer.1 = (bf16[1,128,1536]{2,1,0:T(8,128)(2,1)}, bf16[1,1536,768]{2,1,0:T(8,128)(2,1)}, bf16[1,1536,768]{2,1,0:T(8,128)(2,1)}, bf16[1,768,1536]{2,1,0:T(8,128)(2,1)}, f32[1,1536]{1,0:T(1,128)}) custom-call(bf16[1,128,1536]{2,1,0:T(8,128)(2,1)} %tokens.1, bf16[1,128,1536]{2,1,0:T(8,128)(2,1)} %upstream.1, bf16[1,1536,768]{2,1,0:T(8,128)(2,1)} %gate_w.1, ...), custom_call_target="tpu_custom_call" | custom-call | tf_op jit(solution)/shard_map/layer/pallas_call | solution.py:518
  135.2 6.8 %hand_over.1 = (bf16[1,128,1536]{2,1,0:T(8,128)(2,1)}, bf16[1,1536,768]{2,1,0:T(8,128)(2,1)}, bf16[1,1536,768]{2,1,0:T(8,128)(2,1)}, bf16[1,768,1536]{2,1,0:T(8,128)(2,1)}, f32[1,1536]{1,0:T(1,128)}) custom-call(bf16[1,128,1536]{2,1,0:T(8,128)(2,1)} %get-tuple-element.10.refs_0_, bf16[1,1536,768]{2,1,0:T(8,128)(2,1)} %get-tuple-element.11.refs_1_, ...), custom_call_target="tpu_custom_call" | custom-call | tf_op jit(solution)/shard_map/hand_over/pallas_call | solution.py:549

commit v7 on v5

--- a/solution.py
+++ b/solution.py
@@ -23,24 +23,24 @@
 BASE = tuple(N * first for first in FIRST)
 
 ORDER = (
-    ("E1", 0), ("N", 1), ("E1", 2), ("N", 2), ("E1", 1), ("E5", 0), ("E3", 0), ("E3", 1), ("E5", 2),
-    ("E2", 1), ("E5", 1), ("E2", 0), ("E6", 0), ("E4", 0), ("E3", 2), ("E1", 3), ("E7", 0), ("E6", 1),
-    ("O1", 0), ("O2", 0), ("E6", 2), ("E2", 2), ("P1", 0), ("E1", 4), ("E4", 1), ("E7", 1), ("P2", 0),
-    ("P4", 0), ("E4", 2), ("E7", 2), ("E3", 3), ("O1", 1), ("E5", 3), ("E2", 3), ("P1", 1), ("P2", 1),
-    ("P4", 1), ("E6", 3), ("E4", 3), ("E3", 4), ("E2", 4), ("P1", 2), ("P2", 2), ("E7", 3), ("P4", 2),
-    ("N", 3), ("E5", 4), ("N", 4), ("F0", 0), ("O2", 1), ("F0", 1), ("E6", 4), ("O1", 2), ("F2", 1),
-    ("F2", 0), ("F2b", 0), ("E4", 4), ("P1", 3), ("P2", 3), ("P4", 3), ("E7", 4), ("F3", 1), ("F2b", 1),
-    ("F3", 0), ("O2", 2), ("F0", 2), ("O1", 3), ("P1", 4), ("F2", 2), ("P2", 4), ("F2b", 2), ("F4", 1),
-    ("O2", 3), ("F4", 0), ("F3", 2), ("F0", 3), ("P4", 4), ("O1", 4), ("G3", 1), ("O2", 4), ("F4", 2),
-    ("G3", 0), ("G5", 1), ("F2", 3), ("G2", 1), ("G2", 0), ("G2", 2), ("F2b", 3), ("G5", 0), ("G6", 0),
-    ("G6", 1), ("G4", 1), ("F0", 4), ("G7", 0), ("G4", 0), ("F3", 3), ("B1", 0), ("G3", 2), ("B2", 0),
-    ("G7", 1), ("F2", 4), ("F2b", 4), ("B1", 1), ("F4", 3), ("G4", 2), ("F3", 4), ("G5", 2), ("S2", 0),
-    ("B2", 1), ("G2", 3), ("S2b", 0), ("G6", 2), ("G3", 3), ("G7", 2), ("B1", 2), ("F4", 4), ("G4", 3),
-    ("B2", 2), ("G5", 4), ("G3", 4), ("G2", 4), ("S2", 1), ("S3", 0), ("G5", 3), ("S2b", 1), ("G6", 3),
-    ("G7", 3), ("S2b", 2), ("B1", 3), ("G4", 4), ("S2", 2), ("B2", 3), ("S3", 1), ("G6", 4), ("G7", 4),
-    ("B1", 4), ("B2", 4), ("S2", 3), ("S2b", 3), ("WD", 2), ("S3", 2), ("B4", 4), ("S4", 1), ("WU", 4),
-    ("S2", 4), ("S3", 3), ("WD", 0), ("WU", 2), ("S2b", 4), ("WD", 1), ("S4", 0), ("S4", 2), ("S4", 3),
-    ("S3", 4), ("K1", 0), ("WU", 3), ("WU", 0), ("WU", 5), ("WU", 1), ("S4", 4), ("K2", 0),
+    ("E1", 0), ("E1", 1), ("E1", 2), ("N", 1), ("N", 2), ("E2", 0), ("E5", 0), ("E5", 1), ("E3", 0),
+    ("E3", 1), ("E5", 2), ("E6", 0), ("E3", 2), ("E4", 0), ("E7", 0), ("E2", 1), ("E6", 1), ("E2", 2),
+    ("O1", 0), ("E1", 3), ("E4", 1), ("O2", 0), ("E6", 2), ("P1", 0), ("P2", 0), ("E7", 1), ("E4", 2),
+    ("P4", 0), ("E7", 2), ("E3", 3), ("E1", 4), ("E5", 3), ("O1", 1), ("P1", 1), ("P2", 1), ("P4", 1),
+    ("E3", 4), ("E2", 3), ("N", 3), ("P1", 2), ("E6", 3), ("P2", 2), ("E4", 3), ("P4", 2), ("E2", 4),
+    ("F0", 0), ("O2", 1), ("F0", 1), ("E7", 3), ("O1", 2), ("E5", 4), ("E6", 4), ("O1", 3), ("F2", 0),
+    ("F2", 1), ("P1", 3), ("P2", 3), ("F3", 0), ("E7", 4), ("F3", 1), ("E4", 4), ("F2b", 1), ("P4", 3),
+    ("F2b", 0), ("N", 4), ("O2", 2), ("F0", 2), ("O2", 3), ("P1", 4), ("F2", 2), ("F4", 0), ("F2b", 2),
+    ("P2", 4), ("F4", 1), ("F3", 2), ("F0", 3), ("P4", 4), ("G2", 0), ("G3", 1), ("G2", 1), ("G3", 0),
+    ("F2b", 3), ("F4", 2), ("O1", 4), ("G5", 1), ("G5", 0), ("G4", 0), ("G6", 0), ("F2", 3), ("G6", 1),
+    ("O2", 4), ("G5", 2), ("F0", 4), ("G2", 2), ("G7", 1), ("G4", 1), ("F3", 3), ("G7", 0), ("B1", 0),
+    ("G3", 2), ("B2", 0), ("F2", 4), ("B1", 1), ("G4", 2), ("F2b", 4), ("F4", 3), ("F3", 4), ("B2", 1),
+    ("G2", 3), ("F4", 4), ("G5", 3), ("G3", 3), ("G6", 2), ("G7", 2), ("G4", 3), ("S2", 1), ("B1", 2),
+    ("G2", 4), ("B2", 2), ("G3", 4), ("G6", 3), ("S2", 0), ("G4", 4), ("S2b", 0), ("S2", 2), ("S3", 1),
+    ("G5", 4), ("S2b", 1), ("S2b", 2), ("G7", 3), ("B1", 3), ("S3", 0), ("B2", 3), ("G7", 4), ("G6", 4),
+    ("B1", 4), ("S4", 0), ("B2", 4), ("S2", 3), ("S2b", 3), ("B4", 4), ("WD", 2), ("S3", 2), ("WU", 5),
+    ("WD", 0), ("S3", 3), ("S2", 4), ("WD", 1), ("WU", 4), ("WU", 2), ("S2b", 4), ("S4", 1), ("S4", 2),
+    ("S4", 3), ("K1", 0), ("S3", 4), ("WU", 0), ("WU", 1), ("WU", 3), ("S4", 4), ("K2", 0),
 )
 
 

time: 137 us -> 137 us (level)
  no operation moved by 1% of the time
where the time goes in v7:
time: 137 us
  Pallas kernels  136 us (99%)
    pallas_call x1, Pallas kernels, shards(): pl.pallas_call(kernel, out_shape=results, in_specs=[hbm, hbm, hbm, hbm, h...  130 us
    pallas_call x1, Pallas kernels, shards(): pl.pallas_call(hand_over, out_shape=results, in_specs=[hbm] * 5, out_spec...  6.12 us

profile of v7, /device:TPU:0, one launch (start us, length us, event | category | flops | bytes accessed | tf_op | source)
XLA Modules:
  0.0 136.6 jit_solution(7303648290751599625)
XLA Ops:
  0.6 129.7 %layer.1 = (bf16[1,128,1536]{2,1,0:T(8,128)(2,1)}, bf16[1,1536,768]{2,1,0:T(8,128)(2,1)}, bf16[1,1536,768]{2,1,0:T(8,128)(2,1)}, bf16[1,768,1536]{2,1,0:T(8,128)(2,1)}, f32[1,1536]{1,0:T(1,128)}) custom-call(bf16[1,128,1536]{2,1,0:T(8,128)(2,1)} %tokens.1, bf16[1,128,1536]{2,1,0:T(8,128)(2,1)} %upstream.1, bf16[1,1536,768]{2,1,0:T(8,128)(2,1)} %gate_w.1, ...), custom_call_target="tpu_custom_call" | custom-call | tf_op jit(solution)/shard_map/layer/pallas_call | solution.py:515
  130.3 6.1 %hand_over.1 = (bf16[1,128,1536]{2,1,0:T(8,128)(2,1)}, bf16[1,1536,768]{2,1,0:T(8,128)(2,1)}, bf16[1,1536,768]{2,1,0:T(8,128)(2,1)}, bf16[1,768,1536]{2,1,0:T(8,128)(2,1)}, f32[1,1536]{1,0:T(1,128)}) custom-call(bf16[1,128,1536]{2,1,0:T(8,128)(2,1)} %get-tuple-element.10.refs_0_, bf16[1,1536,768]{2,1,0:T(8,128)(2,1)} %get-tuple-element.11.refs_1_, ...), custom_call_target="tpu_custom_call" | custom-call | tf_op jit(solution)/shard_map/hand_over/pallas_call | solution.py:546
